TPU v7x, 32 devices: a whole 2x2x4 slice. The times are simulated.
32 devices in a mesh: freq: 8 (over z, y), sta: 4 (over x, core).
Axes of the slice: x: 2, y: 2, z: 4, core: 2. Of those that a mesh axis runs over, the one named last changes fastest.
Arguments:
- spectra: float32 [2, 128, 64, 8192], P(None, 'freq', None, 'sta'), may hold values from -24 to 24
- current: float32 [64, 2, 128, 512], P('freq', None, None, 'sta'), may hold values from -600 to 600, as said below
- previous: float32 [64, 2, 128, 512], P('freq', None, None, 'sta'), may hold values from -600 to 600, as said below
- table: int32 [64, 512], replicated, may hold values from 0 to 16383
- station_block: int32 [8192], P('sta'), may hold values from 0 to 63
- offsets: float32 [2, 8192], P(None, 'sta'), may hold values from -4 to 4
- slowness: float32 [2, 512], replicated, may hold values from -3 to 3
- weights: float32 [512], P('sta'), may hold values from 400 to 5000
- momentum: float32 [1], replicated, may hold values from 2 to 10
Outputs:
- estimate: float32 [64, 2, 128, 512], P('freq', None, None, 'sta')
- extrapolated: float32 [64, 2, 128, 512], P('freq', None, None, 'sta')
Inputs may be any that keep to these rules, and one draw needn't show every extreme that they name: `current`: real values. `previous`: real values.
All inputs are finite; a program needn't handle non-finite values.
Results may differ from a plain program's by a relative error of at most 0.00105.
The roundings to bfloat16 on the way count: a program that leaves them out, or rounds other values in their place, can miss the bound.
Values may be sent and summed in bfloat16 or wider, within the bound.
A program may use at most 192 MiB of HBM per device.

v0:
```python
import math

import jax
import jax.numpy as jnp
from jax import lax
from jax.sharding import PartitionSpec as P

F = 64
CELLS = 512


def cell_block(cell_count):
    block_len = cell_count
    while block_len > 512 and block_len % 2 == 0:
        block_len = block_len // 2
    return block_len


def phases(number, delay_rows, off_rows, slow_cols, period):
    wrapped = number * delay_rows % period
    geometry = (
        off_rows[0][:, None] * slow_cols[0][None, :] + off_rows[1][:, None] * slow_cols[1][None, :]
    )
    phase_angle = (wrapped.astype(jnp.float32) + number.astype(jnp.float32) * geometry) * (
        2.0 * math.pi / period
    )
    return (jnp.cos(phase_angle).astype(jnp.bfloat16), jnp.sin(phase_angle).astype(jnp.bfloat16))


def forward_terms(cos_part, sin_part, iterate):
    window_count = iterate.shape[1]
    stacked = iterate.reshape(2 * window_count, iterate.shape[2])
    contract = (((1,), (1,)), ((), ()))
    with_cos = lax.dot_general(stacked, cos_part, contract, preferred_element_type=jnp.float32)
    with_sin = lax.dot_general(stacked, sin_part, contract, preferred_element_type=jnp.float32)
    real_part = with_cos[:window_count] + with_sin[window_count:]
    imag_part = with_cos[window_count:] - with_sin[:window_count]
    return jnp.stack([real_part, imag_part])


def adjoint_terms(cos_part, sin_part, residual):
    window_count = residual.shape[1]
    stacked = residual.reshape(2 * window_count, residual.shape[2])
    with_cos = jnp.dot(stacked, cos_part, preferred_element_type=jnp.float32)
    with_sin = jnp.dot(stacked, sin_part, preferred_element_type=jnp.float32)
    real_part = with_cos[:window_count] - with_sin[window_count:]
    imag_part = with_cos[window_count:] + with_sin[:window_count]
    return jnp.stack([real_part, imag_part])


def local(spectra, current, previous, table, station_block, offsets, slowness, weights, momentum):
    period = 4 * F
    normalizer = 1.0 / math.sqrt(CELLS)
    bin_count = current.shape[0]
    cell_share = current.shape[3]
    stations_here = station_block.shape[0]
    station_total = stations_here * lax.axis_size("sta")
    first_bin = lax.axis_index("freq") * bin_count
    relaid = lax.all_to_all(
        spectra.astype(jnp.bfloat16), "freq", split_axis=2, concat_axis=1, tiled=True
    ).astype(spectra.dtype)
    iterate_b = current.astype(jnp.bfloat16)
    segment = lax.all_gather(iterate_b, "sta", axis=3, tiled=True)
    cell_count = segment.shape[3]
    block_len = cell_block(cell_count)
    delay_rows = jnp.take(table, station_block, axis=0)
    bin_terms = []
    cos_blocks = []
    sin_blocks = []
    for add_bin_index in range(bin_count):
        cos_part, sin_part = phases(
            first_bin + add_bin_index + 1, delay_rows, offsets, slowness, period
        )
        cos_blocks.append(cos_part)
        sin_blocks.append(sin_part)
        bin_terms.append(
            forward_terms(cos_part, sin_part, segment[add_bin_index, :, :, 0:block_len])
        )
    running = jnp.stack(bin_terms)
    cos_all = jnp.stack(cos_blocks)
    sin_all = jnp.stack(sin_blocks)
    predicted, cos_all, sin_all = (running, cos_all, sin_all)
    bin_sums = []
    for bin_index in range(bin_count):
        residual = (predicted[bin_index] * normalizer - relaid[:, :, bin_index, :]).astype(
            jnp.bfloat16
        )
        bin_sums.append(
            adjoint_terms(cos_all[bin_index], sin_all[bin_index], residual) * normalizer
        )
    partial_sums = jnp.stack(bin_sums)
    summed = lax.psum(partial_sums, "sta")
    gradient = lax.dynamic_slice_in_dim(summed, lax.axis_index("sta") * cell_share, cell_share, 3)
    step_size = CELLS / (math.sqrt(station_total) + math.sqrt(CELLS)) ** 2
    stepped = current - step_size * gradient
    threshold = step_size * weights
    squares = jnp.sum(stepped * stepped, axis=(0, 1))
    group_norm = jnp.sqrt(lax.psum(squares, "freq") + 1e-06)
    estimate = stepped * jnp.maximum(0.0, 1.0 - threshold[None, :] / group_norm)
    momentum_now = momentum[0]
    momentum_next = (1.0 + jnp.sqrt(1.0 + 4.0 * momentum_now * momentum_now)) / 2.0
    extrapolated = estimate + (momentum_now - 1.0) / momentum_next * (estimate - previous)
    return (estimate, extrapolated)


def solution(mesh):
    in_specs = (
        P(None, "freq", None, "sta"),
        P("freq", None, None, "sta"),
        P("freq", None, None, "sta"),
        P(),
        P("sta"),
        P(None, "sta"),
        P(),
        P("sta"),
        P(),
    )
    out_specs = (P("freq", None, None, "sta"), P("freq", None, None, "sta"))
    return jax.shard_map(local, mesh=mesh, in_specs=in_specs, out_specs=out_specs, check_vma=False)
```

profile of v0, /device:TPU:0, one launch (start us, length us, event | category | flops | bytes accessed | tf_op | source)
XLA Modules:
  0.0 836.4 jit_solution(6741037382420943036)
XLA Ops:
  7.2 2.1 convert_element_type.149
  9.4 17.2 %copy.25 = bf16[2,16,64,2048]{3,1,0,2:T(8,128)(2,1)} copy(f32[2,16,64,2048]{3,2,1,0:T(8,128)} %param.9) | data formatting | bytes 25165824 | tf_op args[0]
  26.6 7.4 all-to-all-start
  34.4 8.9 %gather_fusion = s32[2048,512]{1,0:T(8,128)} fusion(s32[64,512]{1,0:T(8,128)S(1)} %copy-done, s32[2048]{0:T(1024)S(1)} %fusion.96), kind=kCustom, calls=%fused_computation | custom fusion | bytes 8396800 | tf_op jit(solution)/shard_map/jit(_take)/gather | solution.py:66
  43.3 18.0 %fusion.31 = (f32[2048,512]{1,0:T(8,128)}, f32[2048,512]{1,0:T(8,128)}, f32[2048,512]{1,0:T(8,128)}, f32[2048,512]{1,0:T(8,128)}, f32[2048,512]{1,0:T(8,128)}, /*index=5*/f32[2048,512]{1,0:T(8,128)}) fusion(s32[2048,512]{1,0:T(8,128)} %gather_fusion, f32[]{:T(128)S(6)} %convert_element_type.188, s32[]{:T(128)S(6)} %add.230, f32[512]{0:T(512)S(1)} %bitcast.221, ...), kind=kLoop, calls=%fused_computation.58 | loop fusion | flops 104857600 | bytes 29382704 | tf_op jit(solution)/shard_map/mul | solution.py:24
  61.3 8.7 %fusion.27 = (f32[2048,512]{1,0:T(8,128)}, f32[2048,512]{1,0:T(8,128)}) fusion(s32[2048,512]{1,0:T(8,128)} %gather_fusion, f32[]{:T(128)S(6)} %convert_element_type.183, s32[]{:T(128)S(6)} %add.225, f32[512]{0:T(512)S(1)} %bitcast.222, f32[2048]{0:T(1024)S(1)} %bitcast.218, f32[512]{0:T(512)S(1)} %bitcast.220, f32[2048]{0:T(1024)S(1)} %bitcast.216, ...), kind=kLoop, calls=%fused_computation.54 | loop fusion | flops 37748736 | bytes 12605456 | tf_op jit(solution)/shard_map/mul | solution.py:24
  70.0 1.8 fusion.98
  72.8 15.0 %convolution_bitcast_fusion.2 = f32[256,2048]{1,0:T(8,128)S(1)} fusion(bf16[256,512]{1,0:T(8,128)(2,1)S(1)} %bitcast.213, f32[2048,512]{1,0:T(8,128)S(1)} %copy-done.16), kind=kOutput, calls=%fused_computation.78 | convolution fusion | flops 537919488 | bytes 6553600 | tf_op jit(solution)/shard_map/dot_general | solution.py:35
  87.8 14.9 %convolution_bitcast_fusion.3 = f32[256,2048]{1,0:T(8,128)S(1)} fusion(bf16[256,512]{1,0:T(8,128)(2,1)S(1)} %bitcast.214, f32[2048,512]{1,0:T(8,128)S(1)} %copy-done.16), kind=kOutput, calls=%fused_computation.79 | convolution fusion | flops 537919488 | bytes 6553600 | tf_op jit(solution)/shard_map/dot_general | solution.py:34
  105.7 15.0 %convolution_bitcast_fusion.14 = f32[256,2048]{1,0:T(8,128)S(1)} fusion(bf16[256,512]{1,0:T(8,128)(2,1)S(1)} %bitcast.211, f32[2048,512]{1,0:T(8,128)S(1)} %copy-done.14), kind=kOutput, calls=%fused_computation.90 | convolution fusion | flops 537919488 | bytes 6553600 | tf_op jit(solution)/shard_map/dot_general | solution.py:35
  120.7 15.1 %convolution_bitcast_fusion.15 = f32[256,2048]{1,0:T(8,128)S(1)} fusion(bf16[256,512]{1,0:T(8,128)(2,1)S(1)} %bitcast.212, f32[2048,512]{1,0:T(8,128)S(1)} %copy-done.14), kind=kOutput, calls=%fused_computation.91 | convolution fusion | flops 537919488 | bytes 6553600 | tf_op jit(solution)/shard_map/dot_general | solution.py:34
  137.7 15.0 %convolution_bitcast_fusion = f32[256,2048]{1,0:T(8,128)S(1)} fusion(bf16[256,512]{1,0:T(8,128)(2,1)S(1)} %bitcast.209, f32[2048,512]{1,0:T(8,128)S(1)} %copy-done.12), kind=kOutput, calls=%fused_computation.76 | convolution fusion | flops 537919488 | bytes 6553600 | tf_op jit(solution)/shard_map/dot_general | solution.py:35
  152.7 14.9 %convolution_bitcast_fusion.1 = f32[256,2048]{1,0:T(8,128)S(1)} fusion(bf16[256,512]{1,0:T(8,128)(2,1)S(1)} %bitcast.210, f32[2048,512]{1,0:T(8,128)S(1)} %copy-done.12), kind=kOutput, calls=%fused_computation.77 | convolution fusion | flops 537919488 | bytes 6553600 | tf_op jit(solution)/shard_map/dot_general | solution.py:34
  167.9 1.7 maximum_multiply_fusion.7
  169.6 15.0 %convolution_bitcast_fusion.12 = f32[256,2048]{1,0:T(8,128)S(1)} fusion(bf16[256,512]{1,0:T(8,128)(2,1)S(1)} %bitcast.207, f32[2048,512]{1,0:T(8,128)S(1)} %copy-done.10), kind=kOutput, calls=%fused_computation.88 | convolution fusion | flops 537919488 | bytes 6553600 | tf_op jit(solution)/shard_map/dot_general | solution.py:35
  184.6 14.9 %convolution_bitcast_fusion.13 = f32[256,2048]{1,0:T(8,128)S(1)} fusion(bf16[256,512]{1,0:T(8,128)(2,1)S(1)} %bitcast.208, f32[2048,512]{1,0:T(8,128)S(1)} %copy-done.10), kind=kOutput, calls=%fused_computation.89 | convolution fusion | flops 537919488 | bytes 6553600 | tf_op jit(solution)/shard_map/dot_general | solution.py:34
  201.4 15.5 %convolution_bitcast_fusion.10 = f32[256,2048]{1,0:T(8,128)S(1)} fusion(bf16[256,512]{1,0:T(8,128)(2,1)S(1)} %bitcast.205, f32[2048,512]{1,0:T(8,128)S(1)} %copy-done.8), kind=kOutput, calls=%fused_computation.86 | convolution fusion | flops 537919488 | bytes 6553600 | tf_op jit(solution)/shard_map/dot_general | solution.py:35
  216.8 14.9 %convolution_bitcast_fusion.11 = f32[256,2048]{1,0:T(8,128)S(1)} fusion(bf16[256,512]{1,0:T(8,128)(2,1)S(1)} %bitcast.206, f32[2048,512]{1,0:T(8,128)S(1)} %copy-done.8), kind=kOutput, calls=%fused_computation.87 | convolution fusion | flops 537919488 | bytes 6553600 | tf_op jit(solution)/shard_map/dot_general | solution.py:34
  233.6 15.0 %convolution_bitcast_fusion.8 = f32[256,2048]{1,0:T(8,128)S(1)} fusion(bf16[256,512]{1,0:T(8,128)(2,1)S(1)} %bitcast.203, f32[2048,512]{1,0:T(8,128)S(1)} %copy-done.6), kind=kOutput, calls=%fused_computation.84 | convolution fusion | flops 537919488 | bytes 6553600 | tf_op jit(solution)/shard_map/dot_general | solution.py:35
  248.7 14.9 %convolution_bitcast_fusion.9 = f32[256,2048]{1,0:T(8,128)S(1)} fusion(bf16[256,512]{1,0:T(8,128)(2,1)S(1)} %bitcast.204, f32[2048,512]{1,0:T(8,128)S(1)} %copy-done.6), kind=kOutput, calls=%fused_computation.85 | convolution fusion | flops 537919488 | bytes 6553600 | tf_op jit(solution)/shard_map/dot_general | solution.py:34
  265.4 15.0 %convolution_bitcast_fusion.6 = f32[256,2048]{1,0:T(8,128)S(1)} fusion(bf16[256,512]{1,0:T(8,128)(2,1)S(1)} %bitcast.201, f32[2048,512]{1,0:T(8,128)S(1)} %copy-done.4), kind=kOutput, calls=%fused_computation.82 | convolution fusion | flops 537919488 | bytes 6553600 | tf_op jit(solution)/shard_map/dot_general | solution.py:35
  280.5 15.1 %convolution_bitcast_fusion.7 = f32[256,2048]{1,0:T(8,128)S(1)} fusion(bf16[256,512]{1,0:T(8,128)(2,1)S(1)} %bitcast.202, f32[2048,512]{1,0:T(8,128)S(1)} %copy-done.4), kind=kOutput, calls=%fused_computation.83 | convolution fusion | flops 537919488 | bytes 6553600 | tf_op jit(solution)/shard_map/dot_general | solution.py:34
  297.4 15.0 %convolution_bitcast_fusion.4 = f32[256,2048]{1,0:T(8,128)S(1)} fusion(bf16[256,512]{1,0:T(8,128)(2,1)S(1)} %bitcast.199, f32[2048,512]{1,0:T(8,128)S(1)} %copy-done.2), kind=kOutput, calls=%fused_computation.80 | convolution fusion | flops 537919488 | bytes 6553600 | tf_op jit(solution)/shard_map/dot_general | solution.py:35
  312.4 14.9 %convolution_bitcast_fusion.5 = f32[256,2048]{1,0:T(8,128)S(1)} fusion(bf16[256,512]{1,0:T(8,128)(2,1)S(1)} %bitcast.200, f32[2048,512]{1,0:T(8,128)S(1)} %copy-done.2), kind=kOutput, calls=%fused_computation.81 | convolution fusion | flops 537919488 | bytes 6553600 | tf_op jit(solution)/shard_map/dot_general | solution.py:34
  329.2 14.0 %convert_bitcast_fusion = f32[2,8,16,8,2048]{4,3,1,2,0:T(8,128)} fusion(bf16[2,16,64,2048]{3,1,0,2:T(8,128)(2,1)} %all-to-all-done), kind=kLoop, calls=%fused_computation.1 | loop fusion | flops 4194304 | bytes 25165824 | tf_op jit(solution)/shard_map/convert_element_type | solution.py:61
  343.2 11.9 %copy.14 = f32[2,8,16,8,2048]{4,3,2,1,0:T(8,128)} copy(f32[2,8,16,8,2048]{4,3,1,2,0:T(8,128)} %convert_bitcast_fusion) | data formatting | bytes 33554432 | tf_op jit(solution)/shard_map/convert_element_type | solution.py:61
  355.2 59.7 %fusion.97 = (f32[2,128,1,2048]{3,2,1,0:T(1,128)}, f32[2,128,1,2048]{3,2,1,0:T(1,128)}, f32[2,128,1,2048]{3,2,1,0:T(1,128)S(1)}, f32[2,128,1,2048]{3,2,1,0:T(1,1...) fusion(f32[2,128,8,2048]{3,2,1,0:T(8,128)} %bitcast.198), kind=kLoop, calls=%fused_computation.221 | loop fusion | bytes 33554432 | tf_op jit(solution)/shard_map/slice | solution.py:85
  414.9 2.6 copy.21
  418.4 13.8 %fusion.69 = f32[256,512]{1,0:T(8,128)S(1)} fusion(bf16[256,2048]{1,0:T(8,128)(2,1)S(1)} %fusion.33, f32[2048,512]{1,0:T(8,128)S(1)} %copy-done.17), kind=kOutput, calls=%fused_computation.164 | convolution fusion | flops 537919488 | bytes 5767168 | tf_op jit(solution)/shard_map/dot_general | solution.py:45
  432.2 14.1 %fusion.68 = f32[256,512]{1,0:T(8,128)S(1)} fusion(bf16[256,2048]{1,0:T(8,128)(2,1)S(1)} %fusion.33, f32[2048,512]{1,0:T(8,128)S(1)} %copy-done.17), kind=kOutput, calls=%fused_computation.163 | convolution fusion | flops 537919488 | bytes 5767168 | tf_op jit(solution)/shard_map/dot_general | solution.py:44
  448.5 14.0 %fusion.57 = f32[256,512]{1,0:T(8,128)S(1)} fusion(bf16[256,2048]{1,0:T(8,128)(2,1)S(1)} %fusion.39, f32[2048,512]{1,0:T(8,128)S(1)} %copy-done.15), kind=kOutput, calls=%fused_computation.152 | convolution fusion | flops 537919488 | bytes 5767168 | tf_op jit(solution)/shard_map/dot_general | solution.py:45
  462.5 13.9 %fusion.56 = f32[256,512]{1,0:T(8,128)S(1)} fusion(bf16[256,2048]{1,0:T(8,128)(2,1)S(1)} %fusion.39, f32[2048,512]{1,0:T(8,128)S(1)} %copy-done.15), kind=kOutput, calls=%fused_computation.151 | convolution fusion | flops 537919488 | bytes 5767168 | tf_op jit(solution)/shard_map/dot_general | solution.py:44
  478.7 14.0 %fusion.71 = f32[256,512]{1,0:T(8,128)S(1)} fusion(bf16[256,2048]{1,0:T(8,128)(2,1)S(1)} %fusion.32, f32[2048,512]{1,0:T(8,128)S(1)} %copy-done.13), kind=kOutput, calls=%fused_computation.166 | convolution fusion | flops 537919488 | bytes 5767168 | tf_op jit(solution)/shard_map/dot_general | solution.py:45
  492.7 14.2 %fusion.70 = f32[256,512]{1,0:T(8,128)S(1)} fusion(bf16[256,2048]{1,0:T(8,128)(2,1)S(1)} %fusion.32, f32[2048,512]{1,0:T(8,128)S(1)} %copy-done.13), kind=kOutput, calls=%fused_computation.165 | convolution fusion | flops 537919488 | bytes 5767168 | tf_op jit(solution)/shard_map/dot_general | solution.py:44
  509.1 14.0 %fusion.59 = f32[256,512]{1,0:T(8,128)S(1)} fusion(bf16[256,2048]{1,0:T(8,128)(2,1)S(1)} %fusion.38, f32[2048,512]{1,0:T(8,128)S(1)} %copy-done.11), kind=kOutput, calls=%fused_computation.154 | convolution fusion | flops 537919488 | bytes 5767168 | tf_op jit(solution)/shard_map/dot_general | solution.py:45
  523.1 13.9 %fusion.58 = f32[256,512]{1,0:T(8,128)S(1)} fusion(bf16[256,2048]{1,0:T(8,128)(2,1)S(1)} %fusion.38, f32[2048,512]{1,0:T(8,128)S(1)} %copy-done.11), kind=kOutput, calls=%fused_computation.153 | convolution fusion | flops 537919488 | bytes 5767168 | tf_op jit(solution)/shard_map/dot_general | solution.py:44
  539.2 14.0 %fusion.61 = f32[256,512]{1,0:T(8,128)S(1)} fusion(bf16[256,2048]{1,0:T(8,128)(2,1)S(1)} %fusion.37, f32[2048,512]{1,0:T(8,128)S(1)} %copy-done.9), kind=kOutput, calls=%fused_computation.156 | convolution fusion | flops 537919488 | bytes 5767168 | tf_op jit(solution)/shard_map/dot_general | solution.py:45
  553.3 14.2 %fusion.60 = f32[256,512]{1,0:T(8,128)S(1)} fusion(bf16[256,2048]{1,0:T(8,128)(2,1)S(1)} %fusion.37, f32[2048,512]{1,0:T(8,128)S(1)} %copy-done.9), kind=kOutput, calls=%fused_computation.155 | convolution fusion | flops 537919488 | bytes 5767168 | tf_op jit(solution)/shard_map/dot_general | solution.py:44
  569.7 14.0 %fusion.63 = f32[256,512]{1,0:T(8,128)S(1)} fusion(bf16[256,2048]{1,0:T(8,128)(2,1)S(1)} %fusion.36, f32[2048,512]{1,0:T(8,128)S(1)} %copy-done.7), kind=kOutput, calls=%fused_computation.158 | convolution fusion | flops 537919488 | bytes 5767168 | tf_op jit(solution)/shard_map/dot_general | solution.py:45
  583.7 13.9 %fusion.62 = f32[256,512]{1,0:T(8,128)S(1)} fusion(bf16[256,2048]{1,0:T(8,128)(2,1)S(1)} %fusion.36, f32[2048,512]{1,0:T(8,128)S(1)} %copy-done.7), kind=kOutput, calls=%fused_computation.157 | convolution fusion | flops 537919488 | bytes 5767168 | tf_op jit(solution)/shard_map/dot_general | solution.py:44
  599.8 14.0 %fusion.65 = f32[256,512]{1,0:T(8,128)S(1)} fusion(bf16[256,2048]{1,0:T(8,128)(2,1)S(1)} %fusion.35, f32[2048,512]{1,0:T(8,128)S(1)} %copy-done.5), kind=kOutput, calls=%fused_computation.160 | convolution fusion | flops 537919488 | bytes 5767168 | tf_op jit(solution)/shard_map/dot_general | solution.py:45
  613.9 14.2 %fusion.64 = f32[256,512]{1,0:T(8,128)S(1)} fusion(bf16[256,2048]{1,0:T(8,128)(2,1)S(1)} %fusion.35, f32[2048,512]{1,0:T(8,128)S(1)} %copy-done.5), kind=kOutput, calls=%fused_computation.159 | convolution fusion | flops 537919488 | bytes 5767168 | tf_op jit(solution)/shard_map/dot_general | solution.py:44
  630.2 14.0 %fusion.67 = f32[256,512]{1,0:T(8,128)S(1)} fusion(bf16[256,2048]{1,0:T(8,128)(2,1)S(1)} %fusion.34, f32[2048,512]{1,0:T(8,128)S(1)} %copy-done.3), kind=kOutput, calls=%fused_computation.162 | convolution fusion | flops 537919488 | bytes 5767168 | tf_op jit(solution)/shard_map/dot_general | solution.py:45
  644.2 13.9 %fusion.66 = f32[256,512]{1,0:T(8,128)S(1)} fusion(bf16[256,2048]{1,0:T(8,128)(2,1)S(1)} %fusion.34, f32[2048,512]{1,0:T(8,128)S(1)} %copy-done.3), kind=kOutput, calls=%fused_computation.161 | convolution fusion | flops 537919488 | bytes 5767168 | tf_op jit(solution)/shard_map/dot_general | solution.py:44
  665.9 87.0 %all-reduce.3.cloned.1.call-done = f32[8,2,128,512]{3,2,1,0:T(8,128)} async-done(((f32[8,2,128,512]{3,2,1,0:T(8,128)}), f32[8,2,128,512]{3,2,1,0:T(8,128)}) %all-reduce.3.cloned.1.call-update) | async-done | bytes 4194320 | tf_op jit(solution)/shard_map/psum | solution.py:92
  752.9 2.0 multiply_reduce_fusion
  755.6 70.3 %all-reduce.5.cloned.1.call-done = f32[128,128]{1,0:T(8,128)} async-done(((f32[128,128]{1,0:T(8,128)}), f32[128,128]{1,0:T(8,128)}) %all-reduce.5.cloned.1.call-update) | async-done | bytes 65552 | tf_op jit(solution)/shard_map/psum | solution.py:98
  826.8 2.8 multiply_add_fusion.1
  (136 shorter events, 40.3 us)
Async XLA Ops:
  7.2 27.2 %copy-start = (s32[64,512]{1,0:T(8,128)S(1)}, s32[64,512]{1,0:T(8,128)}, u32[]{:S(2)}) copy-start(s32[64,512]{1,0:T(8,128)} %param.12) | copy-start | bytes 393220
  7.2 62.8 %all-gather.2.cloned.1.call-start = ((), (), s32[]{:S(2)}) async-start(), calls=%async_computation.1 | async-start | bytes 2621440 | tf_op jit(solution)/shard_map/all_gather | solution.py:63
  26.6 7.7 copy-start.34
  26.6 7.7 copy-start.36
  26.6 7.8 copy-start.35
  26.6 302.7 %all-to-all-start = ((bf16[2,16,64,2048]{3,1,0,2:T(8,128)(2,1)}), bf16[2,16,64,2048]{3,1,0,2:T(8,128)(2,1)}, u32[]{:S(2)}, u32[]{:S(2)}) async-start(bf16[2,16,64,2048]{3,1,0,2:T(8,128)(2,1)} %copy.25), calls=%async_computation | async-start | bytes 16777216 | tf_op jit(solution)/shard_map/all_to_all | solution.py:59
  34.0 718.8 %all-reduce.3.cloned.1.call-start = ((), (), s32[]{:S(2)}) async-start(), calls=%async_computation.2 | async-start | bytes 8388608 | tf_op jit(solution)/shard_map/psum | solution.py:92
  70.0 2.8 copy-start.16
  102.7 2.9 copy-start.14
  120.7 17.0 %copy-start.12 = (f32[2048,512]{1,0:T(8,128)S(1)}, f32[2048,512]{1,0:T(8,128)}, u32[]{:S(2)}) copy-start(f32[2048,512]{1,0:T(8,128)} %get-tuple-element.12) | copy-start | bytes 12582916
  152.7 16.9 %copy-start.10 = (f32[2048,512]{1,0:T(8,128)S(1)}, f32[2048,512]{1,0:T(8,128)}, u32[]{:S(2)}) copy-start(f32[2048,512]{1,0:T(8,128)} %get-tuple-element.13) | copy-start | bytes 12582916
  184.6 16.7 %copy-start.8 = (f32[2048,512]{1,0:T(8,128)S(1)}, f32[2048,512]{1,0:T(8,128)}, u32[]{:S(2)}) copy-start(f32[2048,512]{1,0:T(8,128)} %get-tuple-element.14) | copy-start | bytes 12582916
  216.8 16.8 %copy-start.6 = (f32[2048,512]{1,0:T(8,128)S(1)}, f32[2048,512]{1,0:T(8,128)}, u32[]{:S(2)}) copy-start(f32[2048,512]{1,0:T(8,128)} %get-tuple-element.15) | copy-start | bytes 12582916
  248.7 16.8 %copy-start.4 = (f32[2048,512]{1,0:T(8,128)S(1)}, f32[2048,512]{1,0:T(8,128)}, u32[]{:S(2)}) copy-start(f32[2048,512]{1,0:T(8,128)} %get-tuple-element.16) | copy-start | bytes 12582916
  280.4 17.0 %copy-start.2 = (f32[2048,512]{1,0:T(8,128)S(1)}, f32[2048,512]{1,0:T(8,128)}, u32[]{:S(2)}) copy-start(f32[2048,512]{1,0:T(8,128)} %get-tuple-element.17) | copy-start | bytes 12582916
  414.9 2.7 copy-start.25
  414.9 3.4 copy-start.17
  432.2 14.1 %copy-start.24 = (f32[2,128,1,2048]{3,2,1,0:T(1,128)S(1)}, f32[2,128,1,2048]{3,2,1,0:T(1,128)}, u32[]{:S(2)}) copy-start(f32[2,128,1,2048]{3,2,1,0:T(1,128)} %get-tuple-element.11) | copy-start | bytes 6291460
  432.2 15.1 %copy-start.26 = (f32[2,128,2048]{2,1,0:T(8,128)S(1)}, f32[2,128,2048]{2,1,0:T(8,128)}, u32[]{:S(2)}) copy-start(f32[2,128,2048]{2,1,0:T(8,128)} %maximum_multiply_fusion) | copy-start | bytes 6291460
  446.3 2.2 copy-start.15
  462.5 13.9 %copy-start.23 = (f32[2,128,1,2048]{3,2,1,0:T(1,128)S(1)}, f32[2,128,1,2048]{3,2,1,0:T(1,128)}, u32[]{:S(2)}) copy-start(f32[2,128,1,2048]{3,2,1,0:T(1,128)} %get-tuple-element.4) | copy-start | bytes 6291460
  462.5 14.9 %copy-start.27 = (f32[2,128,2048]{2,1,0:T(8,128)S(1)}, f32[2,128,2048]{2,1,0:T(8,128)}, u32[]{:S(2)}) copy-start(f32[2,128,2048]{2,1,0:T(8,128)} %maximum_multiply_fusion.7) | copy-start | bytes 6291460
  476.5 2.2 copy-start.13
  492.7 14.2 %copy-start.22 = (f32[2,128,1,2048]{3,2,1,0:T(1,128)S(1)}, f32[2,128,1,2048]{3,2,1,0:T(1,128)}, u32[]{:S(2)}) copy-start(f32[2,128,1,2048]{3,2,1,0:T(1,128)} %get-tuple-element.10) | copy-start | bytes 6291460
  492.7 15.1 %copy-start.28 = (f32[2,128,2048]{2,1,0:T(8,128)S(1)}, f32[2,128,2048]{2,1,0:T(8,128)}, u32[]{:S(2)}) copy-start(f32[2,128,2048]{2,1,0:T(8,128)} %maximum_multiply_fusion.1) | copy-start | bytes 6291460
  506.9 2.2 copy-start.11
  523.1 13.9 %copy-start.21 = (f32[2,128,1,2048]{3,2,1,0:T(1,128)S(1)}, f32[2,128,1,2048]{3,2,1,0:T(1,128)}, u32[]{:S(2)}) copy-start(f32[2,128,1,2048]{3,2,1,0:T(1,128)} %get-tuple-element.9) | copy-start | bytes 6291460
  523.1 14.9 %copy-start.29 = (f32[2,128,2048]{2,1,0:T(8,128)S(1)}, f32[2,128,2048]{2,1,0:T(8,128)}, u32[]{:S(2)}) copy-start(f32[2,128,2048]{2,1,0:T(8,128)} %maximum_multiply_fusion.2) | copy-start | bytes 6291460
  537.0 2.2 copy-start.9
  553.3 14.2 %copy-start.20 = (f32[2,128,1,2048]{3,2,1,0:T(1,128)S(1)}, f32[2,128,1,2048]{3,2,1,0:T(1,128)}, u32[]{:S(2)}) copy-start(f32[2,128,1,2048]{3,2,1,0:T(1,128)} %get-tuple-element.8) | copy-start | bytes 6291460
  553.3 15.1 %copy-start.30 = (f32[2,128,2048]{2,1,0:T(8,128)S(1)}, f32[2,128,2048]{2,1,0:T(8,128)}, u32[]{:S(2)}) copy-start(f32[2,128,2048]{2,1,0:T(8,128)} %maximum_multiply_fusion.3) | copy-start | bytes 6291460
  567.5 2.2 copy-start.7
  583.7 13.9 %copy-start.19 = (f32[2,128,1,2048]{3,2,1,0:T(1,128)S(1)}, f32[2,128,1,2048]{3,2,1,0:T(1,128)}, u32[]{:S(2)}) copy-start(f32[2,128,1,2048]{3,2,1,0:T(1,128)} %get-tuple-element.7) | copy-start | bytes 6291460
  583.7 14.9 %copy-start.31 = (f32[2,128,2048]{2,1,0:T(8,128)S(1)}, f32[2,128,2048]{2,1,0:T(8,128)}, u32[]{:S(2)}) copy-start(f32[2,128,2048]{2,1,0:T(8,128)} %maximum_multiply_fusion.4) | copy-start | bytes 6291460
  597.6 2.2 copy-start.5
  613.9 15.1 %copy-start.32 = (f32[2,128,2048]{2,1,0:T(8,128)S(1)}, f32[2,128,2048]{2,1,0:T(8,128)}, u32[]{:S(2)}) copy-start(f32[2,128,2048]{2,1,0:T(8,128)} %maximum_multiply_fusion.5) | copy-start | bytes 6291460
  628.0 2.2 copy-start.3
  662.3 90.6 %copy-start.18 = (f32[8,2,128,128]{3,2,1,0:T(8,128)S(1)}, f32[8,2,128,128]{3,2,1,0:T(8,128)}, u32[]{:S(2)}) copy-start(f32[8,2,128,128]{3,2,1,0:T(8,128)} %param.10) | copy-start | bytes 3145732
  664.0 90.9 %copy-start.37 = (f32[128]{0:T(128)S(1)}, f32[128]{0:T(128)}, u32[]{:S(2)}) copy-start(f32[128]{0:T(128)} %param.16) | copy-start | bytes 1540
  664.0 162.8 %copy-start.33 = (f32[8,2,128,128]{3,2,1,0:T(8,128)S(1)}, f32[8,2,128,128]{3,2,1,0:T(8,128)}, u32[]{:S(2)}) copy-start(f32[8,2,128,128]{3,2,1,0:T(8,128)} %param.11) | copy-start | bytes 3145732
  665.8 163.8 %copy-start.1 = (s32[64,512]{1,0:T(8,128)S(1)}, s32[64,512]{1,0:T(8,128)}, u32[]{:S(2)}) copy-start(s32[64,512]{1,0:T(8,128)} %param.12) | copy-start | bytes 393220
  665.8 160.0 %all-reduce.5.cloned.1.call-start = ((), (), s32[]{:S(2)}) async-start(), calls=%async_computation.3 | async-start | bytes 131072 | tf_op jit(solution)/shard_map/psum | solution.py:98
Sparse Core Ops, SparseCore 0:
  10.1 25.5 all-gather.1
  666.0 86.8 all-reduce.2
  757.2 68.6 all-reduce.4
where the time goes:
time: 841 us; the launch traced here: 836 us
  matrix products  464 us (55%)
  waiting for transfers between devices  157 us (19%)
  local copies, waits for them, and re-layouts  118 us (14%)
  other arithmetic  73.5 us (9%)
  between operations  15.7 us (2%)
    dot_general x8, matrix products, forward_terms(): lax.dot_general(stacked, sin_part, contract, preferred_element_type=jnp.f...  120 us
    dot_general x8, matrix products, forward_terms(): lax.dot_general(stacked, cos_part, contract, preferred_element_type=jnp.f...  120 us
    dot_general x8, matrix products, adjoint_terms(): with_cos = jnp.dot(stacked, cos_part, preferred_element_type=jnp.float32)  112 us
    dot_general x8, matrix products, adjoint_terms(): with_sin = jnp.dot(stacked, sin_part, preferred_element_type=jnp.float32)  112 us
    psum x1, waiting for transfers between devices, local(): summed = lax.psum(partial_sums, 'sta')  87 us
    psum x1, waiting for transfers between devices, local(): group_norm = jnp.sqrt(lax.psum(squares, 'freq') + 1e-06)  70.3 us
    slice x1, local copies, waits for them, and re-layouts, local(): relaid[:, :, bin_index, :]  59.7 us
    unnamed x85, local copies, waits for them, and re-layouts  35.6 us
  transfers between devices with their start and end apart: 4, of which 2 were waited for; matrix products, arithmetic and copies ran while one was open for 37% of the time, Pallas kernels for 0%

commit v1 on v0

--- a/solution.py
+++ b/solution.py
@@ -1,8 +1,11 @@
+import functools
 import math
 
 import jax
 import jax.numpy as jnp
 from jax import lax
+from jax.experimental import pallas as pl
+from jax.experimental.pallas import tpu as pltpu
 from jax.sharding import PartitionSpec as P
 
 F = 64
@@ -103,7 +106,204 @@
     return (estimate, extrapolated)
 
 
+SIN_TERMS = (3.1415926535362892, -5.167712764624382, 2.5501633189428987, -0.5992521977810126, 0.08205040162239277, -0.007028386120383206)
+COS_TERMS = (0.9999999997799041, -4.934802137078749, 4.058709159554242, -1.335212003029471, 0.23493731372678894, -0.024396324214549327)
+
+
+def horner(terms, u):
+    total = jnp.full_like(u, terms[-1])
+    for term in terms[-2::-1]:
+        total = total * u + term
+    return total
+
+
+def turns_cos_sin(turns):
+    part = turns - jnp.round(turns)
+    square = part * part
+    half_sin = part * horner(SIN_TERMS, square)
+    half_cos = horner(COS_TERMS, square)
+    doubled = half_sin + half_sin
+    return 1.0 - doubled * half_sin, doubled * half_cos
+
+
+def bins_kernel(
+    period, normalizer, place_ref, blocks_ref, off_ref, tab_ref, slow_ref, x_ref, o0, o1, o2, o3, g_ref,
+    delay_ref, cos_ref, sin_ref, pred_ref, res_ref
+):
+    bins, cells, tile = cos_ref.shape
+    number = place_ref[0].astype(jnp.float32)
+    spot = place_ref[1]
+    windows = x_ref.shape[1] // 2
+    piece = o0.shape[2]
+    step = pl.program_id(0)
+
+    @pl.when(step == 0)
+    def _():
+        g_ref[...] = jnp.zeros_like(g_ref)
+
+    rows = lax.broadcasted_iota(jnp.int32, (tab_ref.shape[1], tile), 0)
+    picks = jnp.where(rows == blocks_ref[...], 1.0, 0.0).astype(jnp.bfloat16)
+    delay_ref[...] = jnp.dot(tab_ref[...], picks, preferred_element_type=jnp.float32)
+    scale = 1.0 / period
+    strip = 16
+    lanes = 256
+
+    def fill(index, _):
+        row = pl.ds(pl.multiple_of(index // (tile // lanes) * strip, strip), strip)
+        col = pl.ds(pl.multiple_of(index % (tile // lanes) * lanes, lanes), lanes)
+        slow = slow_ref[row, :]
+        geometry = off_ref[0:1, col] * slow[:, 0:1] + off_ref[1:2, col] * slow[:, 1:2]
+        delay = delay_ref[row, col]
+        unit_cos, unit_sin = turns_cos_sin((delay + geometry) * scale)
+        turns = number * delay * scale
+        turns = (turns - jnp.round(turns)) + number * geometry * scale
+        cos_old, sin_old = turns_cos_sin(turns)
+        cos_ref[0, row, col] = cos_old.astype(jnp.bfloat16)
+        sin_ref[0, row, col] = sin_old.astype(jnp.bfloat16)
+        cos_now = cos_old * unit_cos - sin_old * unit_sin
+        sin_now = sin_old * unit_cos + cos_old * unit_sin
+        twice = unit_cos + unit_cos
+        for b in range(1, bins):
+            cos_ref[b, row, col] = cos_now.astype(jnp.bfloat16)
+            sin_ref[b, row, col] = sin_now.astype(jnp.bfloat16)
+            if b < bins - 1:
+                cos_now, cos_old = twice * cos_now - cos_old, cos_now
+                sin_now, sin_old = twice * sin_now - sin_old, sin_now
+        return 0
+
+    lax.fori_loop(0, cells // strip * (tile // lanes), fill, 0)
+
+    across = (((1,), (1,)), ((), ()))
+
+    for b in range(bins):
+        stacked = x_ref[b]
+        with_cos = jnp.dot(stacked, cos_ref[b], preferred_element_type=jnp.float32)
+        with_sin = jnp.dot(stacked, sin_ref[b], preferred_element_type=jnp.float32)
+        pred_ref[b, 0:windows] = (with_cos[:windows] + with_sin[windows:]) * normalizer
+        pred_ref[b, windows:] = (with_cos[windows:] - with_sin[:windows]) * normalizer
+        for d, o_ref in enumerate((o0, o1, o2, o3)):
+            first = jnp.bitwise_xor(spot, d) * piece
+            for k in range(2):
+                at = pl.ds(pl.multiple_of(first + k * windows, piece), piece)
+                res_ref[b, at, :] = (pred_ref[b, at, :] - o_ref[b, k].astype(jnp.float32)).astype(jnp.bfloat16)
+        residual = res_ref[b]
+        back_cos = lax.dot_general(residual, cos_ref[b], across, preferred_element_type=jnp.float32)
+        back_sin = lax.dot_general(residual, sin_ref[b], across, preferred_element_type=jnp.float32)
+        g_ref[b, 0:windows] += back_cos[:windows] - back_sin[windows:]
+        g_ref[b, windows:] += back_cos[windows:] + back_sin[:windows]
+
+
+def bins_gradient(place, blocks, offsets, tab, slow, iterate, observed, period, normalizer):
+    bins, rows, cells = iterate.shape
+    stations = blocks.shape[1]
+    piece = observed[0].shape[2]
+    tile = 512
+    vm = pltpu.VMEM
+    whole = lambda shape: pl.BlockSpec(shape, lambda i: (0,) * len(shape))
+    return pl.pallas_call(
+        functools.partial(bins_kernel, period, normalizer),
+        grid=(stations // tile,),
+        out_shape=jax.ShapeDtypeStruct((bins, rows, cells), jnp.float32),
+        in_specs=[
+            pl.BlockSpec(memory_space=pltpu.SMEM),
+            pl.BlockSpec((1, tile), lambda i: (0, i)),
+            pl.BlockSpec((2, tile), lambda i: (0, i)),
+            whole(tab.shape),
+            whole(slow.shape),
+            whole(iterate.shape),
+        ]
+        + [pl.BlockSpec((bins, 2, piece, tile), lambda i: (0, 0, 0, i))] * 4,
+        out_specs=whole((bins, rows, cells)),
+        scratch_shapes=[
+            vm((cells, tile), jnp.float32),
+            vm((bins, cells, tile), jnp.bfloat16),
+            vm((bins, cells, tile), jnp.bfloat16),
+            vm((bins, rows, tile), jnp.float32),
+            vm((bins, rows, tile), jnp.bfloat16),
+        ],
+        compiler_params=pltpu.CompilerParams(vmem_limit_bytes=52 * 2**20),
+        cost_estimate=pl.CostEstimate(
+            flops=8 * bins * rows * cells * stations, bytes_accessed=16 * 2**20, transcendentals=0
+        ),
+    )(place, blocks, offsets, tab, slow, iterate, *observed)
+
+
+def local_grouped(freq_size, sta_size, spectra, current, previous, table, station_block, offsets, slowness, weights, momentum):
+    period = 4 * F
+    normalizer = 1.0 / math.sqrt(CELLS)
+    bins = current.shape[0]
+    cell_share = current.shape[3]
+    half_windows = current.shape[2] // 2
+    stations_here = station_block.shape[0]
+    station_total = stations_here * sta_size
+    me = lax.axis_index("freq")
+    mine = lax.axis_index("sta")
+    half, spot = me // 4, me % 4
+    gradient_back = []
+    rounded = current.astype(jnp.bfloat16)
+    tab = jnp.bitwise_and(table, period - 1).astype(jnp.bfloat16).T
+    slow = slowness.T
+    blocks = station_block.reshape(1, -1)
+    picks = []
+    iterates = []
+    for c in range(2):
+        give = lax.rem(me + c, 2)
+        sent = lax.dynamic_slice_in_dim(rounded, give * half_windows, half_windows, 2)
+        perm = [(f, ((f + c) % 2) * 4 + f // 2) for f in range(freq_size)]
+        got = lax.ppermute(sent, "freq", perm)
+        iterates.append(lax.all_gather(got, "sta", axis=3, tiled=True))
+        gradient_back.append([(b, a) for a, b in perm])
+    observed = []
+    for c in range(2):
+        odd = lax.rem(half + c, 2)
+        parts = []
+        for d in range(4):
+            first = (2 * jnp.bitwise_xor(spot, d) + odd) * bins
+            part = lax.dynamic_slice_in_dim(spectra, first, bins, 2).astype(jnp.bfloat16)
+            part = jnp.transpose(part, (2, 0, 1, 3))
+            if d:
+                part = lax.ppermute(part, "freq", [(f, f ^ d) for f in range(freq_size)])
+            parts.append(part)
+        observed.append(parts)
+    halves = []
+    for c in range(2):
+        odd = lax.rem(half + c, 2)
+        place = jnp.stack([(2 * spot + odd) * bins + 1, spot]).astype(jnp.int32)
+        iterate = iterates[c].reshape(bins, 2 * half_windows, cell_share * sta_size)
+        partial = bins_gradient(
+            place, blocks, offsets, tab, slow, iterate, observed[c], period, normalizer
+        )
+        total = lax.dynamic_slice_in_dim(partial, mine * cell_share, cell_share, 2)
+        for d in range(1, sta_size):
+            sent = lax.dynamic_slice_in_dim(
+                partial, jnp.bitwise_xor(mine, d) * cell_share, cell_share, 2
+            )
+            total = total + lax.ppermute(sent, "sta", [(s, s ^ d) for s in range(sta_size)])
+        home = lax.ppermute(total * normalizer, "freq", gradient_back[c])
+        halves.append(home.reshape(bins, 2, half_windows, cell_share))
+    even = lax.rem(me, 2) == 0
+    gradient = jnp.concatenate(
+        [jnp.where(even, halves[0], halves[1]), jnp.where(even, halves[1], halves[0])], axis=2
+    )
+    step_size = CELLS / (math.sqrt(station_total) + math.sqrt(CELLS)) ** 2
+    stepped = current - step_size * gradient
+    threshold = step_size * weights
+    squares = jnp.sum(stepped * stepped, axis=(0, 1))
+    for d in (1, 2, 4):
+        squares = squares + lax.ppermute(squares, "freq", [(f, f ^ d) for f in range(freq_size)])
+    group_norm = jnp.sqrt(squares + 1e-06)
+    estimate = stepped * jnp.maximum(0.0, 1.0 - threshold[None, :] / group_norm)
+    momentum_now = momentum[0]
+    momentum_next = (1.0 + jnp.sqrt(1.0 + 4.0 * momentum_now * momentum_now)) / 2.0
+    extrapolated = estimate + (momentum_now - 1.0) / momentum_next * (estimate - previous)
+    return (estimate, extrapolated)
+
+
 def solution(mesh):
+    freq_size, sta_size = mesh.shape["freq"], mesh.shape["sta"]
+    body = local
+    if freq_size == 8 and sta_size == 4:
+        body = functools.partial(local_grouped, freq_size, sta_size)
     in_specs = (
         P(None, "freq", None, "sta"),
         P("freq", None, None, "sta"),
@@ -116,4 +316,4 @@
         P(),
     )
     out_specs = (P("freq", None, None, "sta"), P("freq", None, None, "sta"))
-    return jax.shard_map(local, mesh=mesh, in_specs=in_specs, out_specs=out_specs, check_vma=False)
+    return jax.shard_map(body, mesh=mesh, in_specs=in_specs, out_specs=out_specs, check_vma=False)

time: 841 us -> 298 us (0.35)
  matrix products: 464 us -> 0 us
  waiting for transfers between devices: 157 us -> 31.8 us
  Pallas kernels: 0 us -> 118 us
  local copies, waits for them, and re-layouts: 118 us -> 32.2 us
  starting transfers between devices: 7.75 us -> 92.3 us
  other arithmetic: 73.5 us -> 8.5 us
    dot_general x32 -> x0, matrix products: 464 us -> none  [the longest x8 120 us: forward_terms(): lax.dot_general(stacked, sin_part, contract, preferred_element_type=jnp.f...]
    psum x2 -> x0, waiting for transfers between devices: 157 us -> none  [the longest x1 87 us: local(): summed = lax.psum(partial_sums, 'sta')]
    pallas_call x0 -> x2, Pallas kernels: none -> 118 us  [bins_gradient(): pl.pallas_call(functools.partial(bins_kernel, period, normalizer), grid=(...]
    ppermute x0 -> x19, starting transfers between devices: none -> 92.3 us  [the longest x6 57.4 us: local_grouped(): part = lax.ppermute(part, 'freq', [(f, f ^ d) for f in range(freq_size)])]
    slice x4 -> x0, local copies, waits for them, and re-layouts: 61.6 us -> none  [the longest x1 59.7 us: local(): relaid[:, :, bin_index, :]]
    mul x11 -> x3, other arithmetic: 39.1 us -> 3.93 us  [the longest x2 3.93 us: local_grouped(): home = lax.ppermute(total * normalizer, 'freq', gradient_back[c])]
    ppermute x0 -> x19, waiting for transfers between devices: none -> 31.8 us  [the longest x6 18.6 us: local_grouped(): lax.ppermute(sent, 'sta', [(s, s ^ d) for s in range(sta_size)])]
    convert_element_type x10 -> x1, other arithmetic: 18.4 us -> 1.31 us  [local_grouped(): rounded = current.astype(jnp.bfloat16)]
  transfers between devices with their start and end apart: 4 -> 21, of which waited for: 2 -> 6; matrix products, arithmetic and copies ran while one was open for 37% -> 11% of each run, Pallas kernels for 0% -> 40%
where the time goes in v1:
time: 298 us
  Pallas kernels  118 us (40%)
  starting transfers between devices  92.3 us (31%)
  local copies, waits for them, and re-layouts  32.2 us (11%)
  waiting for transfers between devices  31.8 us (11%)
  between operations  15.1 us (5%)
  other arithmetic  8.5 us (3%)
    pallas_call x2, Pallas kernels, bins_gradient(): pl.pallas_call(functools.partial(bins_kernel, period, normalizer), grid=(...  118 us
    ppermute x6, starting transfers between devices, local_grouped(): part = lax.ppermute(part, 'freq', [(f, f ^ d) for f in range(freq_size)])  57.4 us
    ppermute x3, starting transfers between devices, local_grouped(): lax.ppermute(squares, 'freq', [(f, f ^ d) for f in range(freq_size)])  22.1 us
    unnamed x38, local copies, waits for them, and re-layouts  19.4 us
    ppermute x6, waiting for transfers between devices, local_grouped(): lax.ppermute(sent, 'sta', [(s, s ^ d) for s in range(sta_size)])  18.6 us
    dynamic_slice x1, local copies, waits for them, and re-layouts, local_grouped(): lax.dynamic_slice_in_dim(spectra, first, bins, 2).astype(jnp.bfloat16)  8.82 us
    ppermute x3, waiting for transfers between devices, local_grouped(): lax.ppermute(squares, 'freq', [(f, f ^ d) for f in range(freq_size)])  7.51 us
  transfers between devices with their start and end apart: 21, of which 6 were waited for; matrix products, arithmetic and copies ran while one was open for 11% of the time, Pallas kernels for 40%

profile of v1, /device:TPU:0, one launch (start us, length us, event | category | flops | bytes accessed | tf_op | source)
XLA Modules:
  0.0 297.9 jit_solution(659530661706037027)
XLA Ops:
  7.2 1.3 convert_element_type.31
  8.6 4.1 %collective-permute-start.8 = (bf16[8,2,64,128]{3,2,1,0:T(8,128)(2,1)S(1)}, bf16[8,2,64,128]{3,2,1,0:T(8,128)(2,1)S(1)}, u32[]{:S(2)}, u32[]{:S(2)}) collective-permute-start(bf16[8,2,64,128]{3,2,1,0:T(8,128)(2,1)S(1)} %get-tuple-element.21), channel_id=1, source_target_pairs={{0,16},{4,0},{8,20},{12,4},{16,24},{20,8},{24,28},{28,12},{1,17},{... | collective-permute-start | bytes 786440 | tf_op jit(solution)/shard_map/ppermute | solution.py:253
  12.7 5.6 %collective-permute-done.8 = bf16[8,2,64,128]{3,2,1,0:T(8,128)(2,1)S(1)} collective-permute-done((bf16[8,2,64,128]{3,2,1,0:T(8,128)(2,1)S(1)}, bf16[8,2,64,128]{3,2,1,0:T(8,128)(2,1)S(1)}, u32[]{:S(2)}, u32[]{:S(2)}) %collective-permute-start.8) | collective-permute-done | bytes 262176 | tf_op jit(solution)/shard_map/ppermute | solution.py:253
  18.3 0.7 copy-done.10
  19.2 8.8 %constant_dynamic-slice_fusion.11 = (bf16[2,16,8,2048]{3,2,1,0:T(8,128)(2,1)S(1)}, bf16[2,16,8,2048]{3,2,1,0:T(8,128)(2,1)}, bf16[2,16,8,2048]{3,2,1,0:T(8,128)(...) fusion(f32[2,16,64,2048]{3,2,1,0:T(8,128)} %param.9, ...), kind=kLoop, calls=%fused_computation.39 | loop fusion | bytes 16777248 | tf_op jit(solution)/shard_map/dynamic_slice | solution.py:262
  28.0 2.9 copy.70
  30.9 7.9 %collective-permute-start.10 = (bf16[8,2,16,2048]{3,2,1,0:T(8,128)(2,1)}, bf16[8,2,16,2048]{3,2,1,0:T(8,128)(2,1)}, u32[]{:S(2)}, u32[]{:S(2)}) collective-permute-start(bf16[8,2,16,2048]{3,2,1,0:T(8,128)(2,1)} %bitcast.34), channel_id=1, source_target_pairs={{0,8},{4,12},{8,0},{12,4},{16,24},{20,28},{24,16},{28,20},{1,9},{5... | collective-permute-start | bytes 3145736 | tf_op jit(solution)/shard_map/ppermute | solution.py:265
  38.9 1.6 copy.71
  40.4 1.6 copy.69
  42.0 1.5 collective-permute-start.9
  43.5 1.3 collective-permute-start
  44.9 2.9 copy.65
  47.7 46.5 %collective-permute-start.1 = (bf16[8,2,16,2048]{3,2,1,0:T(8,128)(2,1)}, bf16[8,2,16,2048]{3,2,1,0:T(8,128)(2,1)}, u32[]{:S(2)}, u32[]{:S(2)}) collective-permute-start(bf16[8,2,16,2048]{3,2,1,0:T(8,128)(2,1)} %bitcast.29), channel_id=1, source_target_pairs={{0,4},{4,0},{8,12},{12,8},{16,20},{20,16},{24,28},{28,24},{1,5},{5... | collective-permute-start | bytes 3145736 | tf_op jit(solution)/shard_map/ppermute | solution.py:265
  94.2 1.6 copy.66
  95.8 0.6 collective-permute-start.2
  96.4 1.6 copy.68
  97.9 0.1 copy.21
  98.0 0.1 copy.23
  98.2 1.5 copy.67
  99.8 1.5 copy.64
  101.3 0.1 pad_add_fusion.1.place_ref
  101.4 0.9 collective-permute-start.3
  102.5 1.2 copy-done
  103.7 59.1 %shard_map.105 = f32[8,128,512]{2,1,0:T(8,128)} custom-call(s32[2]{0:T(128)S(1)} %pad_add_fusion.1.place_ref, s32[1,2048]{1,0:T(1,128)S(1)} %bitcast.43, f32[2,2048]{1,0:T(2,128)S(1)} %copy-done.2, bf16[512,64]{1,0:T(8,128)(2,1)S(1)} %fusion.9.tab_ref, f32[512,2]{1,0:T(8,128)S(1)} %bitcast.39, bf16[8,128,512]{2,1,0:T(8,128)(2,1)S(1)} %bitcast.41, ...), custom_call_target="tpu_custom_call" | custom-call | flops 8589934592 | bytes 16777216 | tf_op jit(solution)/shard_map/pallas_call | solution.py:203
  162.8 1.5 constant_dynamic-slice_fusion.2
  164.4 1.6 collective-permute-start.13
  165.9 0.3 collective-permute-start.14
  166.2 1.2 copy-done.1
  167.5 58.9 %shard_map.104 = f32[8,128,512]{2,1,0:T(8,128)} custom-call(s32[2]{0:T(128)S(1)} %pad_add_fusion.place_ref, s32[1,2048]{1,0:T(1,128)S(1)} %bitcast.44, f32[2,2048]{1,0:T(2,128)S(1)} %copy-done.2, bf16[512,64]{1,0:T(8,128)(2,1)S(1)} %fusion.9.tab_ref, f32[512,2]{1,0:T(8,128)S(1)} %bitcast.40, bf16[8,128,512]{2,1,0:T(8,128)(2,1)S(1)} %bitcast.42, ...), custom_call_target="tpu_custom_call" | custom-call | flops 8589934592 | bytes 16777216 | tf_op jit(solution)/shard_map/pallas_call | solution.py:203
  226.4 2.5 constant_dynamic-slice_fusion.10
  228.8 0.4 collective-permute-start.4
  229.2 1.5 collective-permute-start.5
  230.8 2.4 add_multiply_fusion
  233.2 2.0 collective-permute-start.15
  235.2 9.1 %collective-permute-done.5 = f32[8,128,128]{2,1,0:T(8,128)} collective-permute-done((f32[8,128,128]{2,1,0:T(8,128)}, f32[8,128,128]{2,1,0:T(8,128)}, u32[]{:S(2)}, u32[]{:S(2)}) %collective-permute-start.5) | collective-permute-done | bytes 524320 | tf_op jit(solution)/shard_map/ppermute | solution.py:281
  244.3 9.5 %collective-permute-done.6 = f32[8,128,128]{2,1,0:T(8,128)S(1)} collective-permute-done((f32[8,128,128]{2,1,0:T(8,128)S(1)}, f32[8,128,128]{2,1,0:T(8,128)S(1)}, u32[]{:S(2)}, u32[]{:S(2)}) %collective-permute-start.6) | collective-permute-done | bytes 524320 | tf_op jit(solution)/shard_map/ppermute | solution.py:281
  253.8 1.5 add_multiply_fusion.1
  255.3 1.4 collective-permute-start.7
  256.8 0.8 copy-done.9
  257.6 1.3 broadcast_select_fusion.1
  258.9 0.1 multiply_reduce_fusion
  259.0 18.1 %collective-permute-start.16 = (f32[128,128]{1,0:T(8,128)S(1)}, f32[128,128]{1,0:T(8,128)S(1)}, u32[]{:S(2)}, u32[]{:S(2)}) collective-permute-start(f32[128,128]{1,0:T(8,128)S(1)} %multiply_reduce_fusion), channel_id=1, source_target_pairs={{0,4},{4,0},{8,12},{12,8},{16,20},{20,16},{24,28},{28,24},{1,5},{5... | collective-permute-start | bytes 196616 | tf_op jit(solution)/shard_map/ppermute | solution.py:293
  277.1 2.2 collective-permute-done.16
  279.3 0.6 collective-permute-start.17
  279.9 3.8 %collective-permute-done.17 = f32[128,128]{1,0:T(8,128)S(1)} collective-permute-done((f32[128,128]{1,0:T(8,128)S(1)}, f32[128,128]{1,0:T(8,128)S(1)}, u32[]{:S(2)}, u32[]{:S(2)}) %collective-permute-start.17) | collective-permute-done | bytes 65568 | tf_op jit(solution)/shard_map/ppermute | solution.py:293
  283.7 3.5 %collective-permute-start.18 = (f32[128,128]{1,0:T(8,128)S(1)}, f32[128,128]{1,0:T(8,128)S(1)}, u32[]{:S(2)}, u32[]{:S(2)}) collective-permute-start(f32[128,128]{1,0:T(8,128)S(1)} %add.167), channel_id=1, source_target_pairs={{0,16},{4,20},{8,24},{12,28},{16,0},{20,4},{24,8},{28,12},{1,17},{... | collective-permute-start | bytes 196616 | tf_op jit(solution)/shard_map/ppermute | solution.py:293
  287.9 1.5 collective-permute-done.18
  289.5 1.6 multiply_add_fusion
  (53 shorter events, 0.5 us)
Async XLA Ops:
  7.2 95.3 %all-gather.5.cloned.1.call-start = ((), (), s32[]{:S(2)}) async-start(), calls=%async_computation.1 | async-start | bytes 1310720 | tf_op jit(solution)/shard_map/all_gather | solution.py:254
  8.6 9.7 %collective-permute-start.8 = (bf16[8,2,64,128]{3,2,1,0:T(8,128)(2,1)S(1)}, bf16[8,2,64,128]{3,2,1,0:T(8,128)(2,1)S(1)}, u32[]{:S(2)}, u32[]{:S(2)}) collective-permute-start(bf16[8,2,64,128]{3,2,1,0:T(8,128)(2,1)S(1)} %get-tuple-element.21), channel_id=1, source_target_pairs={{0,16},{4,0},{8,20},{12,4},{16,24},{20,8},{24,28},{28,12},{1,17},{... | collective-permute-start | bytes 786440 | tf_op jit(solution)/shard_map/ppermute | solution.py:253
  18.3 0.7 copy-start.10
  19.0 147.2 %all-gather.3.cloned.1.call-start = ((), (), s32[]{:S(2)}) async-start(), calls=%async_computation | async-start | bytes 1310720 | tf_op jit(solution)/shard_map/all_gather | solution.py:254
  28.0 10.9 %copy-start.7 = (bf16[2,16,8,2048]{3,2,1,0:T(8,128)(2,1)S(1)}, bf16[2,16,8,2048]{3,2,1,0:T(8,128)(2,1)}, u32[]{:S(2)}) copy-start(bf16[2,16,8,2048]{3,2,1,0:T(8,128)(2,1)} %get-tuple-element.11) | copy-start | bytes 3145732
  28.0 12.4 %copy-start.6 = (bf16[2,16,8,2048]{3,2,1,0:T(8,128)(2,1)S(1)}, bf16[2,16,8,2048]{3,2,1,0:T(8,128)(2,1)}, u32[]{:S(2)}) copy-start(bf16[2,16,8,2048]{3,2,1,0:T(8,128)(2,1)} %get-tuple-element.6) | copy-start | bytes 3145732
  30.9 70.5 %collective-permute-start.10 = (bf16[8,2,16,2048]{3,2,1,0:T(8,128)(2,1)}, bf16[8,2,16,2048]{3,2,1,0:T(8,128)(2,1)}, u32[]{:S(2)}, u32[]{:S(2)}) collective-permute-start(bf16[8,2,16,2048]{3,2,1,0:T(8,128)(2,1)} %bitcast.34), channel_id=1, source_target_pairs={{0,8},{4,12},{8,0},{12,4},{16,24},{20,28},{24,16},{28,20},{1,9},{5... | collective-permute-start | bytes 3145736 | tf_op jit(solution)/shard_map/ppermute | solution.py:265
  40.4 62.0 %collective-permute-start.11 = (bf16[8,2,16,2048]{3,2,1,0:T(8,128)(2,1)}, bf16[8,2,16,2048]{3,2,1,0:T(8,128)(2,1)}, u32[]{:S(2)}, u32[]{:S(2)}) collective-permute-start(bf16[8,2,16,2048]{3,2,1,0:T(8,128)(2,1)} %bitcast.35), channel_id=1, source_target_pairs={{0,12},{4,8},{8,4},{12,0},{16,28},{20,24},{24,20},{28,16},{1,13},{... | collective-permute-start | bytes 3145736 | tf_op jit(solution)/shard_map/ppermute | solution.py:265
  42.0 60.4 %collective-permute-start.9 = (bf16[8,2,16,2048]{3,2,1,0:T(8,128)(2,1)}, bf16[8,2,16,2048]{3,2,1,0:T(8,128)(2,1)}, u32[]{:S(2)}, u32[]{:S(2)}) collective-permute-start(bf16[8,2,16,2048]{3,2,1,0:T(8,128)(2,1)} %bitcast.33), channel_id=1, source_target_pairs={{0,4},{4,0},{8,12},{12,8},{16,20},{20,16},{24,28},{28,24},{1,5},{5... | collective-permute-start | bytes 3145736 | tf_op jit(solution)/shard_map/ppermute | solution.py:265
  43.5 1.4 collective-permute-start
  44.9 49.3 %copy-start.5 = (bf16[2,16,8,2048]{3,2,1,0:T(8,128)(2,1)S(1)}, bf16[2,16,8,2048]{3,2,1,0:T(8,128)(2,1)}, u32[]{:S(2)}) copy-start(bf16[2,16,8,2048]{3,2,1,0:T(8,128)(2,1)} %get-tuple-element.8) | copy-start | bytes 3145732
  47.7 118.2 %collective-permute-start.1 = (bf16[8,2,16,2048]{3,2,1,0:T(8,128)(2,1)}, bf16[8,2,16,2048]{3,2,1,0:T(8,128)(2,1)}, u32[]{:S(2)}, u32[]{:S(2)}) collective-permute-start(bf16[8,2,16,2048]{3,2,1,0:T(8,128)(2,1)} %bitcast.29), channel_id=1, source_target_pairs={{0,4},{4,0},{8,12},{12,8},{16,20},{20,16},{24,28},{28,24},{1,5},{5... | collective-permute-start | bytes 3145736 | tf_op jit(solution)/shard_map/ppermute | solution.py:265
  94.2 3.7 %copy-start.11 = (s32[64,512]{1,0:T(8,128)S(1)}, s32[64,512]{1,0:T(8,128)}, u32[]{:S(2)}) copy-start(s32[64,512]{1,0:T(8,128)} %param.12) | copy-start | bytes 393220
  94.2 3.8 %copy-start.12 = (f32[2,512]{1,0:T(2,128)S(1)}, f32[2,512]{1,0:T(2,128)}, u32[]{:S(2)}) copy-start(f32[2,512]{1,0:T(2,128)} %param.15) | copy-start | bytes 12292
  95.8 70.5 %collective-permute-start.2 = (bf16[8,2,16,2048]{3,2,1,0:T(8,128)(2,1)}, bf16[8,2,16,2048]{3,2,1,0:T(8,128)(2,1)}, u32[]{:S(2)}, u32[]{:S(2)}) collective-permute-start(bf16[8,2,16,2048]{3,2,1,0:T(8,128)(2,1)} %bitcast.30), channel_id=1, source_target_pairs={{0,8},{4,12},{8,0},{12,4},{16,24},{20,28},{24,16},{28,20},{1,9},{5... | collective-permute-start | bytes 3145736 | tf_op jit(solution)/shard_map/ppermute | solution.py:265
  98.2 4.3 %copy-start.2 = (f32[2,2048]{1,0:T(2,128)S(1)}, f32[2,2048]{1,0:T(2,128)}, u32[]{:S(2)}) copy-start(f32[2,2048]{1,0:T(2,128)} %off_ref.3) | copy-start | bytes 49156
  98.2 4.3 %copy-start.3 = (s32[2048]{0:T(1024)S(1)}, s32[2048]{0:T(1024)}, u32[]{:S(2)}) copy-start(s32[2048]{0:T(1024)} %param.13) | copy-start | bytes 24580
  101.4 64.8 %collective-permute-start.3 = (bf16[8,2,16,2048]{3,2,1,0:T(8,128)(2,1)}, bf16[8,2,16,2048]{3,2,1,0:T(8,128)(2,1)}, u32[]{:S(2)}, u32[]{:S(2)}) collective-permute-start(bf16[8,2,16,2048]{3,2,1,0:T(8,128)(2,1)} %bitcast.31), channel_id=1, source_target_pairs={{0,12},{4,8},{8,4},{12,0},{16,28},{20,24},{24,20},{28,16},{1,13},{... | collective-permute-start | bytes 3145736 | tf_op jit(solution)/shard_map/ppermute | solution.py:265
  102.5 1.2 copy-start
  164.3 66.5 %collective-permute-start.12 = (f32[8,128,128]{2,1,0:T(8,128)S(1)}, f32[8,128,128]{2,1,0:T(8,128)}, u32[]{:S(2)}, u32[]{:S(2)}) collective-permute-start(f32[8,128,128]{2,1,0:T(8,128)S(1)} %get-tuple-element.15), channel_id=1, source_target_pairs={{0,1},{1,0},{2,3},{3,2},{4,5},{5,4},{6,7},{7,6},{8,9},{9,8},{10,11... | collective-permute-start | bytes 1572872 | tf_op jit(solution)/shard_map/ppermute | solution.py:281
  164.4 66.4 %collective-permute-start.13 = (f32[8,128,128]{2,1,0:T(8,128)S(1)}, f32[8,128,128]{2,1,0:T(8,128)}, u32[]{:S(2)}, u32[]{:S(2)}) collective-permute-start(f32[8,128,128]{2,1,0:T(8,128)S(1)} %get-tuple-element.17), channel_id=1, source_target_pairs={{0,2},{1,3},{2,0},{3,1},{4,6},{5,7},{6,4},{7,5},{8,10},{9,11},{10,... | collective-permute-start | bytes 1572872 | tf_op jit(solution)/shard_map/ppermute | solution.py:281
  165.9 64.8 %collective-permute-start.14 = (f32[8,128,128]{2,1,0:T(8,128)S(1)}, f32[8,128,128]{2,1,0:T(8,128)}, u32[]{:S(2)}, u32[]{:S(2)}) collective-permute-start(f32[8,128,128]{2,1,0:T(8,128)S(1)} %get-tuple-element.16), channel_id=1, source_target_pairs={{0,3},{1,2},{2,1},{3,0},{4,7},{5,6},{6,5},{7,4},{8,11},{9,10},{10,... | collective-permute-start | bytes 1572872 | tf_op jit(solution)/shard_map/ppermute | solution.py:281
  166.2 1.2 copy-start.1
  228.8 6.4 %collective-permute-start.4 = (f32[8,128,128]{2,1,0:T(8,128)}, f32[8,128,128]{2,1,0:T(8,128)}, u32[]{:S(2)}, u32[]{:S(2)}) collective-permute-start(f32[8,128,128]{2,1,0:T(8,128)} %get-tuple-element.12), channel_id=1, source_target_pairs={{0,1},{1,0},{2,3},{3,2},{4,5},{5,4},{6,7},{7,6},{8,9},{9,8},{10,11... | collective-permute-start | bytes 1572872 | tf_op jit(solution)/shard_map/ppermute | solution.py:281
  229.2 15.1 %collective-permute-start.5 = (f32[8,128,128]{2,1,0:T(8,128)}, f32[8,128,128]{2,1,0:T(8,128)}, u32[]{:S(2)}, u32[]{:S(2)}) collective-permute-start(f32[8,128,128]{2,1,0:T(8,128)} %get-tuple-element.14), channel_id=1, source_target_pairs={{0,2},{1,3},{2,0},{3,1},{4,6},{5,7},{6,4},{7,5},{8,10},{9,11},{10,... | collective-permute-start | bytes 1572872 | tf_op jit(solution)/shard_map/ppermute | solution.py:281
  230.7 23.1 %collective-permute-start.6 = (f32[8,128,128]{2,1,0:T(8,128)S(1)}, f32[8,128,128]{2,1,0:T(8,128)S(1)}, u32[]{:S(2)}, u32[]{:S(2)}) collective-permute-start(f32[8,128,128]{2,1,0:T(8,128)S(1)} %get-tuple-element.13), channel_id=1, source_target_pairs={{0,3},{1,2},{2,1},{3,0},{4,7},{5,6},{6,5},{7,4},{8,11},{9,10},{10,... | collective-permute-start | bytes 1572872 | tf_op jit(solution)/shard_map/ppermute | solution.py:281
  233.2 25.7 %copy-start.4 = (f32[8,2,128,128]{3,2,1,0:T(8,128)S(1)}, f32[8,2,128,128]{3,2,1,0:T(8,128)}, u32[]{:S(2)}) copy-start(f32[8,2,128,128]{3,2,1,0:T(8,128)} %param.10) | copy-start | bytes 3145732
  233.2 23.6 %collective-permute-start.15 = (f32[8,128,128]{2,1,0:T(8,128)}, f32[8,128,128]{2,1,0:T(8,128)S(1)}, u32[]{:S(2)}, u32[]{:S(2)}) collective-permute-start(f32[8,128,128]{2,1,0:T(8,128)} %add_multiply_fusion), channel_id=1, source_target_pairs={{16,0},{0,4},{20,8},{4,12},{24,16},{8,20},{28,24},{12,28},{17,1},{... | collective-permute-start | bytes 1572872 | tf_op jit(solution)/shard_map/ppermute | solution.py:282
  255.3 2.2 collective-permute-start.7
  256.8 30.4 %copy-start.13 = (f32[128]{0:T(128)S(1)}, f32[128]{0:T(128)}, u32[]{:S(2)}) copy-start(f32[128]{0:T(128)} %param.16) | copy-start | bytes 1540
  256.8 32.7 %copy-start.8 = (f32[8,2,128,128]{3,2,1,0:T(8,128)S(1)}, f32[8,2,128,128]{3,2,1,0:T(8,128)}, u32[]{:S(2)}) copy-start(f32[8,2,128,128]{3,2,1,0:T(8,128)} %param.11) | copy-start | bytes 3145732
  256.8 0.8 copy-start.9
  259.0 20.3 %collective-permute-start.16 = (f32[128,128]{1,0:T(8,128)S(1)}, f32[128,128]{1,0:T(8,128)S(1)}, u32[]{:S(2)}, u32[]{:S(2)}) collective-permute-start(f32[128,128]{1,0:T(8,128)S(1)} %multiply_reduce_fusion), channel_id=1, source_target_pairs={{0,4},{4,0},{8,12},{12,8},{16,20},{20,16},{24,28},{28,24},{1,5},{5... | collective-permute-start | bytes 196616 | tf_op jit(solution)/shard_map/ppermute | solution.py:293
  279.3 4.3 %collective-permute-start.17 = (f32[128,128]{1,0:T(8,128)S(1)}, f32[128,128]{1,0:T(8,128)S(1)}, u32[]{:S(2)}, u32[]{:S(2)}) collective-permute-start(f32[128,128]{1,0:T(8,128)S(1)} %add.166), channel_id=1, source_target_pairs={{0,8},{4,12},{8,0},{12,4},{16,24},{20,28},{24,16},{28,20},{1,9},{5... | collective-permute-start | bytes 196616 | tf_op jit(solution)/shard_map/ppermute | solution.py:293
  283.7 5.7 %collective-permute-start.18 = (f32[128,128]{1,0:T(8,128)S(1)}, f32[128,128]{1,0:T(8,128)S(1)}, u32[]{:S(2)}, u32[]{:S(2)}) collective-permute-start(f32[128,128]{1,0:T(8,128)S(1)} %add.167), channel_id=1, source_target_pairs={{0,16},{4,20},{8,24},{12,28},{16,0},{20,4},{24,8},{28,12},{1,17},{... | collective-permute-start | bytes 196616 | tf_op jit(solution)/shard_map/ppermute | solution.py:293
Sparse Core Ops, SparseCore 0:
  19.1 23.3 all-gather.4
  45.0 62.7 all-gather.2

commit v2 on v1

--- a/solution.py
+++ b/solution.py
@@ -171,7 +171,7 @@
                 sin_now, sin_old = twice * sin_now - sin_old, sin_now
         return 0
 
-    lax.fori_loop(0, cells // strip * (tile // lanes), fill, 0)
+    lax.fori_loop(0, cells // strip * (tile // lanes), fill, 0, unroll=2)
 
     across = (((1,), (1,)), ((), ()))
 
@@ -251,7 +251,7 @@
         sent = lax.dynamic_slice_in_dim(rounded, give * half_windows, half_windows, 2)
         perm = [(f, ((f + c) % 2) * 4 + f // 2) for f in range(freq_size)]
         got = lax.ppermute(sent, "freq", perm)
-        iterates.append(lax.all_gather(got, "sta", axis=3, tiled=True))
+        iterates.append(got)
         gradient_back.append([(b, a) for a, b in perm])
     observed = []
     for c in range(2):
@@ -260,10 +260,12 @@
         for d in range(4):
             first = (2 * jnp.bitwise_xor(spot, d) + odd) * bins
             part = lax.dynamic_slice_in_dim(spectra, first, bins, 2).astype(jnp.bfloat16)
-            part = jnp.transpose(part, (2, 0, 1, 3))
-            if d:
-                part = lax.ppermute(part, "freq", [(f, f ^ d) for f in range(freq_size)])
-            parts.append(part)
+            parts.append(jnp.transpose(part, (2, 0, 1, 3)))
+        if c == 0:
+            parts, iterates = lax.optimization_barrier((parts, iterates))
+            iterates = lax.all_gather(jnp.stack(iterates), "sta", axis=4, tiled=True)
+        for d in range(1, 4):
+            parts[d] = lax.ppermute(parts[d], "freq", [(f, f ^ d) for f in range(freq_size)])
         observed.append(parts)
     halves = []
     for c in range(2):

time: 298 us -> 260 us (0.87)
  starting transfers between devices: 92.3 us -> 43.8 us
  waiting for transfers between devices: 31.8 us -> 64.6 us
  Pallas kernels: 118 us -> 96.9 us
  local copies, waits for them, and re-layouts: 32.2 us -> 28.5 us
    ppermute x6, starting transfers between devices: 57.4 us -> 8.58 us  [local_grouped(): lax.ppermute(parts[d], 'freq', [(f, f ^ d) for f in range(freq_size)])]
    ppermute x6, waiting for transfers between devices: 0.02 us -> 38.9 us  [local_grouped(): lax.ppermute(parts[d], 'freq', [(f, f ^ d) for f in range(freq_size)])]
    pallas_call x2, Pallas kernels: 118 us -> 96.9 us  [bins_gradient(): pl.pallas_call(functools.partial(bins_kernel, period, normalizer), grid=(...]
    unnamed x38 -> x28, local copies, waits for them, and re-layouts: 19.4 us -> 7.6 us
    transpose x0 -> x2, local copies, waits for them, and re-layouts: none -> 6.71 us  [local_grouped(): parts.append(jnp.transpose(part, (2, 0, 1, 3)))]
    ppermute x2, waiting for transfers between devices: 5.61 us -> 0.01 us  [local_grouped(): got = lax.ppermute(sent, 'freq', perm)]
  transfers between devices with their start and end apart: 21 -> 20, of which waited for: 6 -> 8; matrix products, arithmetic and copies ran while one was open for 11% -> 12% of each run, Pallas kernels for 40% -> 37%
where the time goes in v2:
time: 260 us; the launch traced here: 259 us
  Pallas kernels  96.9 us (37%)
  waiting for transfers between devices  64.6 us (25%)
  starting transfers between devices  43.8 us (17%)
  local copies, waits for them, and re-layouts  28.5 us (11%)
  between operations  15 us (6%)
  other arithmetic  10.6 us (4%)
    pallas_call x2, Pallas kernels, bins_gradient(): pl.pallas_call(functools.partial(bins_kernel, period, normalizer), grid=(...  96.9 us
    ppermute x6, waiting for transfers between devices, local_grouped(): lax.ppermute(parts[d], 'freq', [(f, f ^ d) for f in range(freq_size)])  38.9 us
    ppermute x3, starting transfers between devices, local_grouped(): lax.ppermute(squares, 'freq', [(f, f ^ d) for f in range(freq_size)])  22 us
    ppermute x6, waiting for transfers between devices, local_grouped(): lax.ppermute(sent, 'sta', [(s, s ^ d) for s in range(sta_size)])  18.4 us
    dynamic_slice x1, local copies, waits for them, and re-layouts, local_grouped(): lax.dynamic_slice_in_dim(spectra, first, bins, 2).astype(jnp.bfloat16)  8.8 us
    ppermute x6, starting transfers between devices, local_grouped(): lax.ppermute(parts[d], 'freq', [(f, f ^ d) for f in range(freq_size)])  8.58 us
    unnamed x28, local copies, waits for them, and re-layouts  7.6 us
    ppermute x3, waiting for transfers between devices, local_grouped(): lax.ppermute(squares, 'freq', [(f, f ^ d) for f in range(freq_size)])  7.31 us
  transfers between devices with their start and end apart: 20, of which 8 were waited for; matrix products, arithmetic and copies ran while one was open for 12% of the time, Pallas kernels for 37%

profile of v2, /device:TPU:0, one launch (start us, length us, event | category | flops | bytes accessed | tf_op | source)
XLA Modules:
  0.0 259.4 jit_solution(16542426072095406937)
XLA Ops:
  7.2 1.3 convert_element_type.35
  8.6 0.7 constant_dynamic-slice_fusion.10
  9.3 3.6 %collective-permute-start = (bf16[8,2,64,128]{3,2,1,0:T(8,128)(2,1)}, bf16[8,2,64,128]{3,2,1,0:T(8,128)(2,1)}, u32[]{:S(2)}, u32[]{:S(2)}) collective-permute-start(bf16[8,2,64,128]{3,2,1,0:T(8,128)(2,1)} %get-tuple-element.35), channel_id=1, source_target_pairs={{0,0},{4,16},{8,4},{12,20},{16,8},{20,24},{24,12},{28,28},{1,1},{5... | collective-permute-start | bytes 786440 | tf_op jit(solution)/shard_map/ppermute | solution.py:253
  12.9 2.9 %collective-permute-start.1 = (bf16[8,2,64,128]{3,2,1,0:T(8,128)(2,1)S(1)}, bf16[8,2,64,128]{3,2,1,0:T(8,128)(2,1)}, u32[]{:S(2)}, u32[]{:S(2)}) collective-permute-start(bf16[8,2,64,128]{3,2,1,0:T(8,128)(2,1)S(1)} %get-tuple-element.34), channel_id=1, source_target_pairs={{0,16},{4,0},{8,20},{12,4},{16,24},{20,8},{24,28},{28,12},{1,17},{... | collective-permute-start | bytes 786440 | tf_op jit(solution)/shard_map/ppermute | solution.py:253
  15.7 8.8 %constant_dynamic-slice_fusion.3 = (bf16[2,16,8,2048]{3,2,1,0:T(8,128)(2,1)S(1)}, bf16[2,16,8,2048]{3,2,1,0:T(8,128)(2,1)}, bf16[2,16,8,2048]{3,2,1,0:T(8,128)(2...) fusion(f32[2,16,64,2048]{3,2,1,0:T(8,128)} %param.9, ...), kind=kLoop, calls=%fused_computation.32 | loop fusion | bytes 16777248 | tf_op jit(solution)/shard_map/dynamic_slice | solution.py:262
  24.5 4.2 %fusion.2 = (bf16[8,2,16,2048]{3,2,1,0:T(8,128)(2,1)}, bf16[8,2,16,2048]{3,2,1,0:T(8,128)(2,1)}) fusion(bf16[2,16,8,2048]{3,2,1,0:T(8,128)(2,1)} %get-tuple-element.21, bf16[2,16,8,2048]{3,2,1,0:T(8,128)(2,1)} %get-tuple-element.20), kind=kLoop, calls=%fused_computation.10 | loop fusion | bytes 4194304 | tf_op jit(solution)/shard_map/transpose | solution.py:263
  28.8 2.5 fusion
  31.3 1.9 pad_maximum_fusion
  33.2 2.8 %copy.66 = bf16[2,16,8,2048]{3,1,0,2:T(8,128)(2,1)} copy(bf16[2,16,8,2048]{3,2,1,0:T(8,128)(2,1)} %get-tuple-element.17) | data formatting | bytes 2097152
  36.0 2.6 collective-permute-start.10
  38.6 1.5 copy.67
  40.1 0.6 copy.65
  40.7 1.5 collective-permute-start.9
  42.3 1.5 copy.64
  43.8 0.1 copy.21
  44.0 0.1 copy.23
  44.1 0.1 pad_add_fusion.1.place_ref
  44.3 0.6 collective-permute-start.2
  45.0 1.9 collective-permute-start.3
  46.9 16.1 %collective-permute-done.10.o2 = bf16[8,2,16,2048]{3,2,1,0:T(8,128)(2,1)} collective-permute-done((bf16[8,2,16,2048]{3,2,1,0:T(8,128)(2,1)}, bf16[8,2,16,2048]{3,2,1,0:T(8,128)(2,1)}, u32[]{:S(2)}, u32[]{:S(2)}) %collective-permute-start.10) | collective-permute-done | bytes 1048608 | tf_op jit(solution)/shard_map/ppermute | solution.py:268
  63.0 1.9 collective-permute-start.4
  64.9 1.7 fusion.10
  66.7 18.8 %collective-permute-done.11.o3 = bf16[8,2,16,2048]{3,2,1,0:T(8,128)(2,1)} collective-permute-done((bf16[8,2,16,2048]{3,2,1,0:T(8,128)(2,1)}, bf16[8,2,16,2048]{3,2,1,0:T(8,128)(2,1)}, u32[]{:S(2)}, u32[]{:S(2)}) %collective-permute-start.11) | collective-permute-done | bytes 1048608 | tf_op jit(solution)/shard_map/ppermute | solution.py:268
  85.5 4.0 %collective-permute-done.9.o1 = bf16[8,2,16,2048]{3,2,1,0:T(8,128)(2,1)} collective-permute-done((bf16[8,2,16,2048]{3,2,1,0:T(8,128)(2,1)S(1)}, bf16[8,2,16,2048]{3,2,1,0:T(8,128)(2,1)}, u32[]{:S(2)}, u32[]{:S(2)}) %collective-permute-start.9) | collective-permute-done | bytes 1048608 | tf_op jit(solution)/shard_map/ppermute | solution.py:268
  89.5 48.5 %shard_map.105 = f32[8,128,512]{2,1,0:T(8,128)} custom-call(s32[2]{0:T(128)S(1)} %pad_add_fusion.1.place_ref, s32[1,2048]{1,0:T(1,128)S(1)} %bitcast.41, f32[2,2048]{1,0:T(2,128)S(1)} %copy-done, bf16[512,64]{1,0:T(8,128)(2,1)S(1)} %fusion.9.tab_ref, f32[512,2]{1,0:T(8,128)S(1)} %bitcast.39, bf16[8,128,512]{2,1,0:T(8,128)(2,1)S(1)} %bitcast.38, ...), custom_call_target="tpu_custom_call" | custom-call | flops 8589934592 | bytes 16777216 | tf_op jit(solution)/shard_map/pallas_call | solution.py:203
  138.0 1.5 constant_dynamic-slice_fusion.2
  139.6 1.5 collective-permute-start.13
  141.1 0.3 collective-permute-start.14
  141.5 48.3 %shard_map.104 = f32[8,128,512]{2,1,0:T(8,128)} custom-call(s32[2]{0:T(128)S(1)} %pad_add_fusion.place_ref, s32[1,2048]{1,0:T(1,128)S(1)} %bitcast.42, f32[2,2048]{1,0:T(2,128)S(1)} %copy-done, bf16[512,64]{1,0:T(8,128)(2,1)S(1)} %fusion.9.tab_ref, f32[512,2]{1,0:T(8,128)S(1)} %bitcast.40, bf16[8,128,512]{2,1,0:T(8,128)(2,1)S(1)} %bitcast.37, ...), custom_call_target="tpu_custom_call" | custom-call | flops 8589934592 | bytes 16777216 | tf_op jit(solution)/shard_map/pallas_call | solution.py:203
  189.8 1.5 constant_dynamic-slice_fusion.9
  191.3 0.4 collective-permute-start.5
  191.7 1.5 collective-permute-start.6
  193.2 0.8 copy-done.7
  194.0 2.4 add_multiply_fusion
  196.4 1.5 collective-permute-start.15
  197.9 8.7 %collective-permute-done.6 = f32[8,128,128]{2,1,0:T(8,128)} collective-permute-done((f32[8,128,128]{2,1,0:T(8,128)S(1)}, f32[8,128,128]{2,1,0:T(8,128)}, u32[]{:S(2)}, u32[]{:S(2)}) %collective-permute-start.6) | collective-permute-done | bytes 524320 | tf_op jit(solution)/shard_map/ppermute | solution.py:283
  206.6 9.7 %collective-permute-done.7 = f32[8,128,128]{2,1,0:T(8,128)} collective-permute-done((f32[8,128,128]{2,1,0:T(8,128)S(1)}, f32[8,128,128]{2,1,0:T(8,128)}, u32[]{:S(2)}, u32[]{:S(2)}) %collective-permute-start.7) | collective-permute-done | bytes 524320 | tf_op jit(solution)/shard_map/ppermute | solution.py:283
  216.2 1.6 add_multiply_fusion.1
  217.9 1.4 collective-permute-start.8
  219.3 1.4 broadcast_select_fusion.1
  220.7 0.1 multiply_reduce_fusion
  220.9 18.2 %collective-permute-start.16 = (f32[128,128]{1,0:T(8,128)S(1)}, f32[128,128]{1,0:T(8,128)S(1)}, u32[]{:S(2)}, u32[]{:S(2)}) collective-permute-start(f32[128,128]{1,0:T(8,128)S(1)} %multiply_reduce_fusion), channel_id=1, source_target_pairs={{0,4},{4,0},{8,12},{12,8},{16,20},{20,16},{24,28},{28,24},{1,5},{5... | collective-permute-start | bytes 196616 | tf_op jit(solution)/shard_map/ppermute | solution.py:295
  239.1 2.2 collective-permute-done.16
  241.3 1.7 collective-permute-start.17
  243.0 2.7 %collective-permute-done.17 = f32[128,128]{1,0:T(8,128)S(1)} collective-permute-done((f32[128,128]{1,0:T(8,128)S(1)}, f32[128,128]{1,0:T(8,128)S(1)}, u32[]{:S(2)}, u32[]{:S(2)}) %collective-permute-start.17) | collective-permute-done | bytes 65568 | tf_op jit(solution)/shard_map/ppermute | solution.py:295
  245.7 2.1 collective-permute-start.18
  248.5 2.4 collective-permute-done.18
  250.9 1.6 multiply_add_fusion
  (44 shorter events, 0.4 us)
Async XLA Ops:
  7.2 57.7 %all-gather.2.cloned.1.call-start = ((), (), s32[]{:S(2)}) async-start(), calls=%async_computation | async-start | bytes 2621440 | tf_op jit(solution)/shard_map/all_gather | solution.py:266
  9.3 22.0 %collective-permute-start = (bf16[8,2,64,128]{3,2,1,0:T(8,128)(2,1)}, bf16[8,2,64,128]{3,2,1,0:T(8,128)(2,1)}, u32[]{:S(2)}, u32[]{:S(2)}) collective-permute-start(bf16[8,2,64,128]{3,2,1,0:T(8,128)(2,1)} %get-tuple-element.35), channel_id=1, source_target_pairs={{0,0},{4,16},{8,4},{12,20},{16,8},{20,24},{24,12},{28,28},{1,1},{5... | collective-permute-start | bytes 786440 | tf_op jit(solution)/shard_map/ppermute | solution.py:253
  12.9 18.4 %collective-permute-start.1 = (bf16[8,2,64,128]{3,2,1,0:T(8,128)(2,1)S(1)}, bf16[8,2,64,128]{3,2,1,0:T(8,128)(2,1)}, u32[]{:S(2)}, u32[]{:S(2)}) collective-permute-start(bf16[8,2,64,128]{3,2,1,0:T(8,128)(2,1)S(1)} %get-tuple-element.34), channel_id=1, source_target_pairs={{0,16},{4,0},{8,20},{12,4},{16,24},{20,8},{24,28},{28,12},{1,17},{... | collective-permute-start | bytes 786440 | tf_op jit(solution)/shard_map/ppermute | solution.py:253
  24.5 4.2 %copy-start.3 = (bf16[2,16,8,2048]{3,2,1,0:T(8,128)(2,1)S(1)}, bf16[2,16,8,2048]{3,2,1,0:T(8,128)(2,1)}, u32[]{:S(2)}) copy-start(bf16[2,16,8,2048]{3,2,1,0:T(8,128)(2,1)} %get-tuple-element.22) | copy-start | bytes 3145732
  24.5 4.2 %copy-start.4 = (bf16[2,16,8,2048]{3,2,1,0:T(8,128)(2,1)S(1)}, bf16[2,16,8,2048]{3,2,1,0:T(8,128)(2,1)}, u32[]{:S(2)}) copy-start(bf16[2,16,8,2048]{3,2,1,0:T(8,128)(2,1)} %get-tuple-element.23) | copy-start | bytes 3145732
  36.0 27.0 %collective-permute-start.10 = (bf16[8,2,16,2048]{3,2,1,0:T(8,128)(2,1)}, bf16[8,2,16,2048]{3,2,1,0:T(8,128)(2,1)}, u32[]{:S(2)}, u32[]{:S(2)}) collective-permute-start(bf16[8,2,16,2048]{3,2,1,0:T(8,128)(2,1)} %bitcast.32), channel_id=1, source_target_pairs={{0,8},{4,12},{8,0},{12,4},{16,24},{20,28},{24,16},{28,20},{1,9},{5... | collective-permute-start | bytes 3145736 | tf_op jit(solution)/shard_map/ppermute | solution.py:268
  40.1 45.4 %collective-permute-start.11 = (bf16[8,2,16,2048]{3,2,1,0:T(8,128)(2,1)}, bf16[8,2,16,2048]{3,2,1,0:T(8,128)(2,1)}, u32[]{:S(2)}, u32[]{:S(2)}) collective-permute-start(bf16[8,2,16,2048]{3,2,1,0:T(8,128)(2,1)} %bitcast.33), channel_id=1, source_target_pairs={{0,12},{4,8},{8,4},{12,0},{16,28},{20,24},{24,20},{28,16},{1,13},{... | collective-permute-start | bytes 3145736 | tf_op jit(solution)/shard_map/ppermute | solution.py:268
  40.1 3.7 %copy-start.8 = (s32[64,512]{1,0:T(8,128)S(1)}, s32[64,512]{1,0:T(8,128)}, u32[]{:S(2)}) copy-start(s32[64,512]{1,0:T(8,128)} %param.12) | copy-start | bytes 393220
  40.1 3.8 %copy-start.9 = (f32[2,512]{1,0:T(2,128)S(1)}, f32[2,512]{1,0:T(2,128)}, u32[]{:S(2)}) copy-start(f32[2,512]{1,0:T(2,128)} %param.15) | copy-start | bytes 12292
  40.7 22.2 %copy-start.6 = (bf16[8,2,16,2048]{3,2,1,0:T(8,128)(2,1)S(1)}, bf16[8,2,16,2048]{3,2,1,0:T(8,128)(2,1)}, u32[]{:S(2)}) copy-start(bf16[8,2,16,2048]{3,2,1,0:T(8,128)(2,1)} %get-tuple-element.13) | copy-start | bytes 3145732
  40.7 48.7 %collective-permute-start.9 = (bf16[8,2,16,2048]{3,2,1,0:T(8,128)(2,1)S(1)}, bf16[8,2,16,2048]{3,2,1,0:T(8,128)(2,1)}, u32[]{:S(2)}, u32[]{:S(2)}) collective-permute-start(bf16[8,2,16,2048]{3,2,1,0:T(8,128)(2,1)S(1)} %bitcast.47), channel_id=1, source_target_pairs={{0,4},{4,0},{8,12},{12,8},{16,20},{20,16},{24,28},{28,24},{1,5},{5... | collective-permute-start | bytes 3145736 | tf_op jit(solution)/shard_map/ppermute | solution.py:268
  44.3 45.2 %copy-start = (f32[2,2048]{1,0:T(2,128)S(1)}, f32[2,2048]{1,0:T(2,128)}, u32[]{:S(2)}) copy-start(f32[2,2048]{1,0:T(2,128)} %off_ref.3) | copy-start | bytes 49156
  44.3 45.2 %copy-start.1 = (s32[2048]{0:T(1024)S(1)}, s32[2048]{0:T(1024)}, u32[]{:S(2)}) copy-start(s32[2048]{0:T(1024)} %param.13) | copy-start | bytes 24580
  44.3 96.8 %collective-permute-start.2 = (bf16[8,2,16,2048]{3,2,1,0:T(8,128)(2,1)}, bf16[8,2,16,2048]{3,2,1,0:T(8,128)(2,1)}, u32[]{:S(2)}, u32[]{:S(2)}) collective-permute-start(bf16[8,2,16,2048]{3,2,1,0:T(8,128)(2,1)} %get-tuple-element.11), channel_id=1, source_target_pairs={{0,4},{4,0},{8,12},{12,8},{16,20},{20,16},{24,28},{28,24},{1,5},{5... | collective-permute-start | bytes 3145736 | tf_op jit(solution)/shard_map/ppermute | solution.py:268
  45.0 96.5 %collective-permute-start.3 = (bf16[8,2,16,2048]{3,2,1,0:T(8,128)(2,1)}, bf16[8,2,16,2048]{3,2,1,0:T(8,128)(2,1)}, u32[]{:S(2)}, u32[]{:S(2)}) collective-permute-start(bf16[8,2,16,2048]{3,2,1,0:T(8,128)(2,1)} %get-tuple-element.12), channel_id=1, source_target_pairs={{0,8},{4,12},{8,0},{12,4},{16,24},{20,28},{24,16},{28,20},{1,9},{5... | collective-permute-start | bytes 3145736 | tf_op jit(solution)/shard_map/ppermute | solution.py:268
  63.0 78.5 %collective-permute-start.4 = (bf16[8,2,16,2048]{3,2,1,0:T(8,128)(2,1)S(1)}, bf16[8,2,16,2048]{3,2,1,0:T(8,128)(2,1)}, u32[]{:S(2)}, u32[]{:S(2)}) collective-permute-start(bf16[8,2,16,2048]{3,2,1,0:T(8,128)(2,1)S(1)} %copy-done.6), channel_id=1, source_target_pairs={{0,12},{4,8},{8,4},{12,0},{16,28},{20,24},{24,20},{28,16},{1,13},{... | collective-permute-start | bytes 3145736 | tf_op jit(solution)/shard_map/ppermute | solution.py:268
  139.5 53.6 %collective-permute-start.12 = (f32[8,128,128]{2,1,0:T(8,128)S(1)}, f32[8,128,128]{2,1,0:T(8,128)S(1)}, u32[]{:S(2)}, u32[]{:S(2)}) collective-permute-start(f32[8,128,128]{2,1,0:T(8,128)S(1)} %get-tuple-element.29), channel_id=1, source_target_pairs={{0,1},{1,0},{2,3},{3,2},{4,5},{5,4},{6,7},{7,6},{8,9},{9,8},{10,11... | collective-permute-start | bytes 1572872 | tf_op jit(solution)/shard_map/ppermute | solution.py:283
  139.6 54.4 %collective-permute-start.13 = (f32[8,128,128]{2,1,0:T(8,128)S(1)}, f32[8,128,128]{2,1,0:T(8,128)}, u32[]{:S(2)}, u32[]{:S(2)}) collective-permute-start(f32[8,128,128]{2,1,0:T(8,128)S(1)} %get-tuple-element.31), channel_id=1, source_target_pairs={{0,2},{1,3},{2,0},{3,1},{4,6},{5,7},{6,4},{7,5},{8,10},{9,11},{10,... | collective-permute-start | bytes 1572872 | tf_op jit(solution)/shard_map/ppermute | solution.py:283
  141.1 52.9 %collective-permute-start.14 = (f32[8,128,128]{2,1,0:T(8,128)S(1)}, f32[8,128,128]{2,1,0:T(8,128)}, u32[]{:S(2)}, u32[]{:S(2)}) collective-permute-start(f32[8,128,128]{2,1,0:T(8,128)S(1)} %get-tuple-element.30), channel_id=1, source_target_pairs={{0,3},{1,2},{2,1},{3,0},{4,7},{5,6},{6,5},{7,4},{8,11},{9,10},{10,... | collective-permute-start | bytes 1572872 | tf_op jit(solution)/shard_map/ppermute | solution.py:283
  191.3 6.6 %collective-permute-start.5 = (f32[8,128,128]{2,1,0:T(8,128)S(1)}, f32[8,128,128]{2,1,0:T(8,128)}, u32[]{:S(2)}, u32[]{:S(2)}) collective-permute-start(f32[8,128,128]{2,1,0:T(8,128)S(1)} %get-tuple-element.24), channel_id=1, source_target_pairs={{0,1},{1,0},{2,3},{3,2},{4,5},{5,4},{6,7},{7,6},{8,9},{9,8},{10,11... | collective-permute-start | bytes 1572872 | tf_op jit(solution)/shard_map/ppermute | solution.py:283
  191.7 14.9 %collective-permute-start.6 = (f32[8,128,128]{2,1,0:T(8,128)S(1)}, f32[8,128,128]{2,1,0:T(8,128)}, u32[]{:S(2)}, u32[]{:S(2)}) collective-permute-start(f32[8,128,128]{2,1,0:T(8,128)S(1)} %get-tuple-element.26), channel_id=1, source_target_pairs={{0,2},{1,3},{2,0},{3,1},{4,6},{5,7},{6,4},{7,5},{8,10},{9,11},{10,... | collective-permute-start | bytes 1572872 | tf_op jit(solution)/shard_map/ppermute | solution.py:283
  193.2 0.8 copy-start.7
  194.0 22.3 %collective-permute-start.7 = (f32[8,128,128]{2,1,0:T(8,128)S(1)}, f32[8,128,128]{2,1,0:T(8,128)}, u32[]{:S(2)}, u32[]{:S(2)}) collective-permute-start(f32[8,128,128]{2,1,0:T(8,128)S(1)} %get-tuple-element.25), channel_id=1, source_target_pairs={{0,3},{1,2},{2,1},{3,0},{4,7},{5,6},{6,5},{7,4},{8,11},{9,10},{10,... | collective-permute-start | bytes 1572872 | tf_op jit(solution)/shard_map/ppermute | solution.py:283
  196.4 24.3 %copy-start.2 = (f32[8,2,128,128]{3,2,1,0:T(8,128)S(1)}, f32[8,2,128,128]{3,2,1,0:T(8,128)}, u32[]{:S(2)}) copy-start(f32[8,2,128,128]{3,2,1,0:T(8,128)} %param.10) | copy-start | bytes 3145732
  196.4 22.9 %collective-permute-start.15 = (f32[8,128,128]{2,1,0:T(8,128)}, f32[8,128,128]{2,1,0:T(8,128)}, u32[]{:S(2)}, u32[]{:S(2)}) collective-permute-start(f32[8,128,128]{2,1,0:T(8,128)} %add_multiply_fusion), channel_id=1, source_target_pairs={{16,0},{0,4},{20,8},{4,12},{24,16},{8,20},{28,24},{12,28},{17,1},{... | collective-permute-start | bytes 1572872 | tf_op jit(solution)/shard_map/ppermute | solution.py:284
  217.9 1.5 collective-permute-start.8
  219.3 28.4 %copy-start.10 = (f32[128]{0:T(128)S(1)}, f32[128]{0:T(128)}, u32[]{:S(2)}) copy-start(f32[128]{0:T(128)} %param.16) | copy-start | bytes 1540
  219.3 31.6 %copy-start.5 = (f32[8,2,128,128]{3,2,1,0:T(8,128)S(1)}, f32[8,2,128,128]{3,2,1,0:T(8,128)}, u32[]{:S(2)}) copy-start(f32[8,2,128,128]{3,2,1,0:T(8,128)} %param.11) | copy-start | bytes 3145732
  220.9 20.4 %collective-permute-start.16 = (f32[128,128]{1,0:T(8,128)S(1)}, f32[128,128]{1,0:T(8,128)S(1)}, u32[]{:S(2)}, u32[]{:S(2)}) collective-permute-start(f32[128,128]{1,0:T(8,128)S(1)} %multiply_reduce_fusion), channel_id=1, source_target_pairs={{0,4},{4,0},{8,12},{12,8},{16,20},{20,16},{24,28},{28,24},{1,5},{5... | collective-permute-start | bytes 196616 | tf_op jit(solution)/shard_map/ppermute | solution.py:295
  241.3 4.3 %collective-permute-start.17 = (f32[128,128]{1,0:T(8,128)S(1)}, f32[128,128]{1,0:T(8,128)S(1)}, u32[]{:S(2)}, u32[]{:S(2)}) collective-permute-start(f32[128,128]{1,0:T(8,128)S(1)} %add.166), channel_id=1, source_target_pairs={{0,8},{4,12},{8,0},{12,4},{16,24},{20,28},{24,16},{28,20},{1,9},{5... | collective-permute-start | bytes 196616 | tf_op jit(solution)/shard_map/ppermute | solution.py:295
  245.7 5.2 %collective-permute-start.18 = (f32[128,128]{1,0:T(8,128)S(1)}, f32[128,128]{1,0:T(8,128)S(1)}, u32[]{:S(2)}, u32[]{:S(2)}) collective-permute-start(f32[128,128]{1,0:T(8,128)S(1)} %add.167), channel_id=1, source_target_pairs={{0,16},{4,20},{8,24},{12,28},{16,0},{20,4},{24,8},{28,12},{1,17},{... | collective-permute-start | bytes 196616 | tf_op jit(solution)/shard_map/ppermute | solution.py:295
Sparse Core Ops, SparseCore 0:
  33.3 23.2 all-gather.1

commit v3 on v2

--- a/solution.py
+++ b/solution.py
@@ -126,21 +126,10 @@
     return 1.0 - doubled * half_sin, doubled * half_cos
 
 
-def bins_kernel(
-    period, normalizer, place_ref, blocks_ref, off_ref, tab_ref, slow_ref, x_ref, o0, o1, o2, o3, g_ref,
-    delay_ref, cos_ref, sin_ref, pred_ref, res_ref
+def angles_kernel(
+    period, numbers_ref, blocks_ref, off_ref, tab_ref, slow_ref, uc_ref, us_ref, ac_ref, as_ref, bc_ref, bs_ref, delay_ref
 ):
-    bins, cells, tile = cos_ref.shape
-    number = place_ref[0].astype(jnp.float32)
-    spot = place_ref[1]
-    windows = x_ref.shape[1] // 2
-    piece = o0.shape[2]
-    step = pl.program_id(0)
-
-    @pl.when(step == 0)
-    def _():
-        g_ref[...] = jnp.zeros_like(g_ref)
-
+    cells, tile = delay_ref.shape
     rows = lax.broadcasted_iota(jnp.int32, (tab_ref.shape[1], tile), 0)
     picks = jnp.where(rows == blocks_ref[...], 1.0, 0.0).astype(jnp.bfloat16)
     delay_ref[...] = jnp.dot(tab_ref[...], picks, preferred_element_type=jnp.float32)
@@ -154,10 +143,62 @@
         slow = slow_ref[row, :]
         geometry = off_ref[0:1, col] * slow[:, 0:1] + off_ref[1:2, col] * slow[:, 1:2]
         delay = delay_ref[row, col]
-        unit_cos, unit_sin = turns_cos_sin((delay + geometry) * scale)
-        turns = number * delay * scale
-        turns = (turns - jnp.round(turns)) + number * geometry * scale
-        cos_old, sin_old = turns_cos_sin(turns)
+        uc_ref[row, col], us_ref[row, col] = turns_cos_sin((delay + geometry) * scale)
+        for c, (cos_out, sin_out) in enumerate(((ac_ref, as_ref), (bc_ref, bs_ref))):
+            number = numbers_ref[c].astype(jnp.float32)
+            turns = number * delay * scale
+            turns = (turns - jnp.round(turns)) + number * geometry * scale
+            cos_out[row, col], sin_out[row, col] = turns_cos_sin(turns)
+        return 0
+
+    lax.fori_loop(0, cells // strip * (tile // lanes), fill, 0, unroll=2)
+
+
+def angles(numbers, blocks, offsets, tab, slow, period):
+    cells = tab.shape[0]
+    stations = blocks.shape[1]
+    tile = 512
+    whole = lambda shape: pl.BlockSpec(shape, lambda i: (0,) * len(shape))
+    return pl.pallas_call(
+        functools.partial(angles_kernel, period),
+        grid=(stations // tile,),
+        out_shape=[jax.ShapeDtypeStruct((cells, stations), jnp.float32)] * 6,
+        in_specs=[
+            pl.BlockSpec(memory_space=pltpu.SMEM),
+            pl.BlockSpec((1, tile), lambda i: (0, i)),
+            pl.BlockSpec((2, tile), lambda i: (0, i)),
+            whole(tab.shape),
+            whole(slow.shape),
+        ],
+        out_specs=[pl.BlockSpec((cells, tile), lambda i: (0, i))] * 6,
+        scratch_shapes=[pltpu.VMEM((cells, tile), jnp.float32)],
+        compiler_params=pltpu.CompilerParams(vmem_limit_bytes=52 * 2**20),
+        cost_estimate=pl.CostEstimate(flops=25 * 10**9, bytes_accessed=24 * cells * stations, transcendentals=0),
+    )(numbers, blocks, offsets, tab, slow)
+
+
+def bins_kernel(
+    normalizer, place_ref, uc_ref, us_ref, fc_ref, fs_ref, x_ref, o0, o1, o2, o3, g_ref,
+    cos_ref, sin_ref, pred_ref, res_ref
+):
+    bins, cells, tile = cos_ref.shape
+    spot = place_ref[0]
+    windows = x_ref.shape[1] // 2
+    piece = o0.shape[2]
+    step = pl.program_id(0)
+
+    @pl.when(step == 0)
+    def _():
+        g_ref[...] = jnp.zeros_like(g_ref)
+
+    strip = 16
+    lanes = 256
+
+    def fill(index, _):
+        row = pl.ds(pl.multiple_of(index // (tile // lanes) * strip, strip), strip)
+        col = pl.ds(pl.multiple_of(index % (tile // lanes) * lanes, lanes), lanes)
+        unit_cos, unit_sin = uc_ref[row, col], us_ref[row, col]
+        cos_old, sin_old = fc_ref[row, col], fs_ref[row, col]
         cos_ref[0, row, col] = cos_old.astype(jnp.bfloat16)
         sin_ref[0, row, col] = sin_old.astype(jnp.bfloat16)
         cos_now = cos_old * unit_cos - sin_old * unit_sin
@@ -193,29 +234,25 @@
         g_ref[b, windows:] += back_cos[windows:] + back_sin[:windows]
 
 
-def bins_gradient(place, blocks, offsets, tab, slow, iterate, observed, period, normalizer):
+def bins_gradient(place, unit, first, iterate, observed, normalizer):
     bins, rows, cells = iterate.shape
-    stations = blocks.shape[1]
+    stations = unit[0].shape[1]
     piece = observed[0].shape[2]
     tile = 512
     vm = pltpu.VMEM
     whole = lambda shape: pl.BlockSpec(shape, lambda i: (0,) * len(shape))
     return pl.pallas_call(
-        functools.partial(bins_kernel, period, normalizer),
+        functools.partial(bins_kernel, normalizer),
         grid=(stations // tile,),
         out_shape=jax.ShapeDtypeStruct((bins, rows, cells), jnp.float32),
         in_specs=[
             pl.BlockSpec(memory_space=pltpu.SMEM),
-            pl.BlockSpec((1, tile), lambda i: (0, i)),
-            pl.BlockSpec((2, tile), lambda i: (0, i)),
-            whole(tab.shape),
-            whole(slow.shape),
-            whole(iterate.shape),
         ]
+        + [pl.BlockSpec((cells, tile), lambda i: (0, i))] * 4
+        + [whole(iterate.shape)]
         + [pl.BlockSpec((bins, 2, piece, tile), lambda i: (0, 0, 0, i))] * 4,
         out_specs=whole((bins, rows, cells)),
         scratch_shapes=[
-            vm((cells, tile), jnp.float32),
             vm((bins, cells, tile), jnp.bfloat16),
             vm((bins, cells, tile), jnp.bfloat16),
             vm((bins, rows, tile), jnp.float32),
@@ -225,7 +262,7 @@
         cost_estimate=pl.CostEstimate(
             flops=8 * bins * rows * cells * stations, bytes_accessed=16 * 2**20, transcendentals=0
         ),
-    )(place, blocks, offsets, tab, slow, iterate, *observed)
+    )(place, *unit, *first, iterate, *observed)
 
 
 def local_grouped(freq_size, sta_size, spectra, current, previous, table, station_block, offsets, slowness, weights, momentum):
@@ -268,12 +305,13 @@
             parts[d] = lax.ppermute(parts[d], "freq", [(f, f ^ d) for f in range(freq_size)])
         observed.append(parts)
     halves = []
+    numbers = jnp.stack([(2 * spot + lax.rem(half + c, 2)) * bins + 1 for c in range(2)]).astype(jnp.int32)
+    trig = angles(numbers, blocks, offsets, tab, slow, period)
+    place = spot.reshape(1).astype(jnp.int32)
     for c in range(2):
-        odd = lax.rem(half + c, 2)
-        place = jnp.stack([(2 * spot + odd) * bins + 1, spot]).astype(jnp.int32)
         iterate = iterates[c].reshape(bins, 2 * half_windows, cell_share * sta_size)
         partial = bins_gradient(
-            place, blocks, offsets, tab, slow, iterate, observed[c], period, normalizer
+            place, trig[0:2], trig[2 * c + 2 : 2 * c + 4], iterate, observed[c], normalizer
         )
         total = lax.dynamic_slice_in_dim(partial, mine * cell_share, cell_share, 2)
         for d in range(1, sta_size):

time: 260 us -> 237 us (0.912)
  waiting for transfers between devices: 64.6 us -> 46.6 us
  Pallas kernels: 96.9 us -> 91.7 us
  local copies, waits for them, and re-layouts: 28.5 us -> 31.3 us
    ppermute x6, waiting for transfers between devices: 38.9 us -> 18.7 us  [local_grouped(): lax.ppermute(parts[d], 'freq', [(f, f ^ d) for f in range(freq_size)])]
    pallas_call x2 -> x3, Pallas kernels: 96.9 us -> 91.7 us  [the longest x2 63.3 us: bins_gradient(): pl.pallas_call(functools.partial(bins_kernel, normalizer), grid=(stations...]
    ppermute x3, starting transfers between devices: 22 us -> 17.4 us  [local_grouped(): lax.ppermute(squares, 'freq', [(f, f ^ d) for f in range(freq_size)])]
    ppermute x2, starting transfers between devices: 2.91 us -> 6.85 us  [local_grouped(): home = lax.ppermute(total * normalizer, 'freq', gradient_back[c])]
    unnamed x28 -> x26, local copies, waits for them, and re-layouts: 7.6 us -> 9.37 us
  transfers between devices with their start and end apart: 20 -> 20, of which waited for: 8 -> 8; matrix products, arithmetic and copies ran while one was open for 12% -> 14% of each run, Pallas kernels for 37% -> 39%
where the time goes in v3:
time: 237 us
  Pallas kernels  91.7 us (39%)
  waiting for transfers between devices  46.6 us (20%)
  starting transfers between devices  42 us (18%)
  local copies, waits for them, and re-layouts  31.3 us (13%)
  between operations  15 us (6%)
  other arithmetic  10.1 us (4%)
    pallas_call x2, Pallas kernels, bins_gradient(): pl.pallas_call(functools.partial(bins_kernel, normalizer), grid=(stations...  63.3 us
    pallas_call x1, Pallas kernels, angles(): pl.pallas_call(functools.partial(angles_kernel, period), grid=(stations /...  28.4 us
    ppermute x6, waiting for transfers between devices, local_grouped(): lax.ppermute(sent, 'sta', [(s, s ^ d) for s in range(sta_size)])  20.2 us
    ppermute x6, waiting for transfers between devices, local_grouped(): lax.ppermute(parts[d], 'freq', [(f, f ^ d) for f in range(freq_size)])  18.7 us
    ppermute x3, starting transfers between devices, local_grouped(): lax.ppermute(squares, 'freq', [(f, f ^ d) for f in range(freq_size)])  17.4 us
    unnamed x26, local copies, waits for them, and re-layouts  9.37 us
    dynamic_slice x1, local copies, waits for them, and re-layouts, local_grouped(): lax.dynamic_slice_in_dim(spectra, first, bins, 2).astype(jnp.bfloat16)  8.79 us
    ppermute x3, waiting for transfers between devices, local_grouped(): lax.ppermute(squares, 'freq', [(f, f ^ d) for f in range(freq_size)])  7.67 us
  transfers between devices with their start and end apart: 20, of which 8 were waited for; matrix products, arithmetic and copies ran while one was open for 14% of the time, Pallas kernels for 39%

profile of v3, /device:TPU:0, one launch (start us, length us, event | category | flops | bytes accessed | tf_op | source)
XLA Modules:
  0.0 236.7 jit_solution(6542546585241593123)
XLA Ops:
  7.2 1.3 convert_element_type.35
  8.6 0.7 constant_dynamic-slice_fusion.10
  9.3 3.6 %collective-permute-start = (bf16[8,2,64,128]{3,2,1,0:T(8,128)(2,1)}, bf16[8,2,64,128]{3,2,1,0:T(8,128)(2,1)}, u32[]{:S(2)}, u32[]{:S(2)}) collective-permute-start(bf16[8,2,64,128]{3,2,1,0:T(8,128)(2,1)} %get-tuple-element.47), channel_id=1, source_target_pairs={{0,0},{4,16},{8,4},{12,20},{16,8},{20,24},{24,12},{28,28},{1,1},{5... | collective-permute-start | bytes 786440 | tf_op jit(solution)/shard_map/ppermute | solution.py:290
  12.9 2.9 %collective-permute-start.1 = (bf16[8,2,64,128]{3,2,1,0:T(8,128)(2,1)S(1)}, bf16[8,2,64,128]{3,2,1,0:T(8,128)(2,1)}, u32[]{:S(2)}, u32[]{:S(2)}) collective-permute-start(bf16[8,2,64,128]{3,2,1,0:T(8,128)(2,1)S(1)} %get-tuple-element.46), channel_id=1, source_target_pairs={{0,16},{4,0},{8,20},{12,4},{16,24},{20,8},{24,28},{28,12},{1,17},{... | collective-permute-start | bytes 786440 | tf_op jit(solution)/shard_map/ppermute | solution.py:290
  15.7 8.8 %constant_dynamic-slice_fusion.3 = (bf16[2,16,8,2048]{3,2,1,0:T(8,128)(2,1)S(1)}, bf16[2,16,8,2048]{3,2,1,0:T(8,128)(2,1)}, bf16[2,16,8,2048]{3,2,1,0:T(8,128)(2...) fusion(f32[2,16,64,2048]{3,2,1,0:T(8,128)} %param.9, ...), kind=kLoop, calls=%fused_computation.32 | loop fusion | bytes 16777248 | tf_op jit(solution)/shard_map/dynamic_slice | solution.py:299
  24.5 4.2 %fusion = (bf16[8,2,16,2048]{3,2,1,0:T(8,128)(2,1)}, bf16[8,2,16,2048]{3,2,1,0:T(8,128)(2,1)}) fusion(bf16[2,16,8,2048]{3,2,1,0:T(8,128)(2,1)} %get-tuple-element.35, bf16[2,16,8,2048]{3,2,1,0:T(8,128)(2,1)} %get-tuple-element.34), kind=kLoop, calls=%fused_computation.8 | loop fusion | bytes 4194304 | tf_op jit(solution)/shard_map/transpose | solution.py:300
  28.7 2.5 %fusion.2 = (bf16[8,2,16,2048]{3,2,1,0:T(8,128)(2,1)}, bf16[8,2,16,2048]{3,2,1,0:T(8,128)(2,1)}) fusion(bf16[2,16,8,2048]{3,2,1,0:T(8,128)(2,1)S(1)} %copy-done.4, bf16[2,16,8,2048]{3,2,1,0:T(8,128)(2,1)S(1)} %copy-done.3), kind=kLoop, calls=%fused_computation.10 | loop fusion | bytes 4194304 | tf_op jit(solution)/shard_map/transpose | solution.py:300
  31.2 1.9 pad_maximum_fusion
  33.1 2.8 %copy.66 = bf16[2,16,8,2048]{3,1,0,2:T(8,128)(2,1)} copy(bf16[2,16,8,2048]{3,2,1,0:T(8,128)(2,1)} %get-tuple-element.29) | data formatting | bytes 2097152
  35.9 2.6 %collective-permute-start.10 = (bf16[8,2,16,2048]{3,2,1,0:T(8,128)(2,1)}, bf16[8,2,16,2048]{3,2,1,0:T(8,128)(2,1)}, u32[]{:S(2)}, u32[]{:S(2)}) collective-permute-start(bf16[8,2,16,2048]{3,2,1,0:T(8,128)(2,1)} %bitcast.32), channel_id=1, source_target_pairs={{0,8},{4,12},{8,0},{12,4},{16,24},{20,28},{24,16},{28,20},{1,9},{5... | collective-permute-start | bytes 3145736 | tf_op jit(solution)/shard_map/ppermute | solution.py:305
  38.5 1.5 copy.67
  40.0 0.6 copy.65
  40.6 1.5 collective-permute-start.9
  42.1 1.0 copy.21
  43.5 28.4 %shard_map.104 = (f32[512,2048]{1,0:T(8,128)}, f32[512,2048]{1,0:T(8,128)}, f32[512,2048]{1,0:T(8,128)}, f32[512,2048]{1,0:T(8,128)}, f32[512,2048]{1,0:T(8,128)}, /*index=5*/f32[512,2048]{1,0:T(8,128)}) custom-call(s32[2]{0:T(128)S(1)} %pad_add_fusion.numbers_ref, s32[1,2048]{1,0:T(1,128)S(1)} %bitcast.40, f32[2,2048]{1,0:T(2,128)S(1)} %copy-done, ...), custom_call_target="tpu_custom_call" | custom-call | flops 24999999488 | bytes 25165824 | tf_op jit(solution)/shard_map/pallas_call | solution.py:162
  71.8 1.5 copy.64
  73.4 0.6 collective-permute-start.2
  74.0 1.9 collective-permute-start.3
  75.9 1.0 collective-permute-start.4
  76.9 1.7 fusion.10
  78.6 6.8 %collective-permute-done.11.o3 = bf16[8,2,16,2048]{3,2,1,0:T(8,128)(2,1)} collective-permute-done((bf16[8,2,16,2048]{3,2,1,0:T(8,128)(2,1)}, bf16[8,2,16,2048]{3,2,1,0:T(8,128)(2,1)}, u32[]{:S(2)}, u32[]{:S(2)}) %collective-permute-start.11) | collective-permute-done | bytes 1048608 | tf_op jit(solution)/shard_map/ppermute | solution.py:305
  85.4 4.0 %collective-permute-done.9.o1 = bf16[8,2,16,2048]{3,2,1,0:T(8,128)(2,1)} collective-permute-done((bf16[8,2,16,2048]{3,2,1,0:T(8,128)(2,1)S(1)}, bf16[8,2,16,2048]{3,2,1,0:T(8,128)(2,1)}, u32[]{:S(2)}, u32[]{:S(2)}) %collective-permute-start.9) | collective-permute-done | bytes 1048608 | tf_op jit(solution)/shard_map/ppermute | solution.py:305
  89.3 31.7 %shard_map.106 = f32[8,128,512]{2,1,0:T(8,128)} custom-call(s32[1]{0:T(128)} %bitcast.place_ref, f32[512,2048]{1,0:T(8,128)} %get-tuple-element.14.uc_ref, f32[512,2048]{1,0:T(8,128)} %get-tuple-element.15.us_ref, f32[512,2048]{1,0:T(8,128)} %get-tuple-element.24.fc_ref, f32[512,2048]{1,0:T(8,128)} %get-tuple-element.25.fs_ref, ...), custom_call_target="tpu_custom_call" | custom-call | flops 8589934592 | bytes 16777216 | tf_op jit(solution)/shard_map/pallas_call | solution.py:244
  121.1 1.5 constant_dynamic-slice_fusion.2
  122.6 1.6 collective-permute-start.13
  124.2 7.9 %collective-permute-done.2.o1 = bf16[8,2,16,2048]{3,2,1,0:T(8,128)(2,1)S(1)} collective-permute-done((bf16[8,2,16,2048]{3,2,1,0:T(8,128)(2,1)}, bf16[8,2,16,2048]{3,2,1,0:T(8,128)(2,1)S(1)}, u32[]{:S(2)}, u32[]{:S(2)}) %collective-permute-start.2) | collective-permute-done | bytes 1048608 | tf_op jit(solution)/shard_map/ppermute | solution.py:305
  132.2 0.9 copy-done.8
  133.1 31.6 %shard_map.105 = f32[8,128,512]{2,1,0:T(8,128)} custom-call(s32[1]{0:T(128)} %bitcast.place_ref, f32[512,2048]{1,0:T(8,128)} %get-tuple-element.14.uc_ref, f32[512,2048]{1,0:T(8,128)} %get-tuple-element.15.us_ref, f32[512,2048]{1,0:T(8,128)} %get-tuple-element.16.fc_ref, f32[512,2048]{1,0:T(8,128)} %get-tuple-element.17.fs_ref, ...), custom_call_target="tpu_custom_call" | custom-call | flops 8589934592 | bytes 16777216 | tf_op jit(solution)/shard_map/pallas_call | solution.py:244
  164.7 2.5 %constant_dynamic-slice_fusion.9 = (f32[8,128,128]{2,1,0:T(8,128)}, f32[8,128,128]{2,1,0:T(8,128)}, f32[8,128,128]{2,1,0:T(8,128)}) fusion(f32[8,128,512]{2,1,0:T(8,128)} %shard_map.105, s32[]{:T(128)S(6)} %select_n.85, s32[]{:T(128)S(6)} %select_n.87, s32[]{:T(128)S(6)} %select_n.86), kind=kLoop, calls=%fused_computation.38 | loop fusion | bytes 3145740 | tf_op jit(solution)/shard_map/dynamic_slice | solution.py:318
  167.2 0.7 collective-permute-start.5
  167.9 0.8 collective-permute-start.6
  168.7 0.5 collective-permute-start.7
  169.3 1.3 add_multiply_fusion
  170.6 1.5 collective-permute-start.15
  172.1 10.9 %collective-permute-done.6 = f32[8,128,128]{2,1,0:T(8,128)} collective-permute-done((f32[8,128,128]{2,1,0:T(8,128)}, f32[8,128,128]{2,1,0:T(8,128)}, u32[]{:S(2)}, u32[]{:S(2)}) %collective-permute-start.6) | collective-permute-done | bytes 524320 | tf_op jit(solution)/shard_map/ppermute | solution.py:321
  183.0 9.3 %collective-permute-done.7 = f32[8,128,128]{2,1,0:T(8,128)} collective-permute-done((f32[8,128,128]{2,1,0:T(8,128)}, f32[8,128,128]{2,1,0:T(8,128)}, u32[]{:S(2)}, u32[]{:S(2)}) %collective-permute-start.7) | collective-permute-done | bytes 524320 | tf_op jit(solution)/shard_map/ppermute | solution.py:321
  192.3 2.4 %add_multiply_fusion.1 = f32[8,128,128]{2,1,0:T(8,128)} fusion(f32[8,128,128]{2,1,0:T(8,128)} %collective-permute-done.7, f32[8,128,128]{2,1,0:T(8,128)} %collective-permute-done.6, f32[8,128,128]{2,1,0:T(8,128)} %collective-permute-done.5, f32[8,128,512]{2,1,0:T(8,128)} %shard_map.105, s32[]{:T(128)S(6)} %select_n.84), kind=kLoop, calls=%fused_computation.23 | loop fusion | flops 524288 | bytes 2621444 | tf_op jit(solution)/shard_map/mul | solution.py:322
  194.7 5.3 %collective-permute-start.8 = (f32[8,128,128]{2,1,0:T(8,128)}, f32[8,128,128]{2,1,0:T(8,128)}, u32[]{:S(2)}, u32[]{:S(2)}) collective-permute-start(f32[8,128,128]{2,1,0:T(8,128)} %add_multiply_fusion.1), channel_id=1, source_target_pairs={{0,0},{16,4},{4,8},{20,12},{8,16},{24,20},{12,24},{28,28},{1,1},{1... | collective-permute-start | bytes 1572872 | tf_op jit(solution)/shard_map/ppermute | solution.py:322
  200.1 0.8 copy-done.6
  200.9 1.3 broadcast_select_fusion.1
  202.2 0.1 multiply_reduce_fusion
  202.4 14.0 %collective-permute-start.16 = (f32[128,128]{1,0:T(8,128)S(1)}, f32[128,128]{1,0:T(8,128)S(1)}, u32[]{:S(2)}, u32[]{:S(2)}) collective-permute-start(f32[128,128]{1,0:T(8,128)S(1)} %multiply_reduce_fusion), channel_id=1, source_target_pairs={{0,4},{4,0},{8,12},{12,8},{16,20},{20,16},{24,28},{28,24},{1,5},{5... | collective-permute-start | bytes 196616 | tf_op jit(solution)/shard_map/ppermute | solution.py:333
  216.3 2.2 collective-permute-done.16
  218.6 1.4 collective-permute-start.17
  220.0 3.0 %collective-permute-done.17 = f32[128,128]{1,0:T(8,128)S(1)} collective-permute-done((f32[128,128]{1,0:T(8,128)S(1)}, f32[128,128]{1,0:T(8,128)S(1)}, u32[]{:S(2)}, u32[]{:S(2)}) %collective-permute-start.17) | collective-permute-done | bytes 65568 | tf_op jit(solution)/shard_map/ppermute | solution.py:333
  222.9 2.0 collective-permute-start.18
  225.7 2.5 %collective-permute-done.18 = f32[128,128]{1,0:T(8,128)S(1)} collective-permute-done((f32[128,128]{1,0:T(8,128)S(1)}, f32[128,128]{1,0:T(8,128)S(1)}, u32[]{:S(2)}, u32[]{:S(2)}) %collective-permute-start.18) | collective-permute-done | bytes 65568 | tf_op jit(solution)/shard_map/ppermute | solution.py:333
  228.2 1.6 multiply_add_fusion
  (42 shorter events, 0.5 us)
Async XLA Ops:
  7.2 69.7 %all-gather.2.cloned.1.call-start = ((), (), s32[]{:S(2)}) async-start(), calls=%async_computation | async-start | bytes 2621440 | tf_op jit(solution)/shard_map/all_gather | solution.py:303
  9.3 21.9 %collective-permute-start = (bf16[8,2,64,128]{3,2,1,0:T(8,128)(2,1)}, bf16[8,2,64,128]{3,2,1,0:T(8,128)(2,1)}, u32[]{:S(2)}, u32[]{:S(2)}) collective-permute-start(bf16[8,2,64,128]{3,2,1,0:T(8,128)(2,1)} %get-tuple-element.47), channel_id=1, source_target_pairs={{0,0},{4,16},{8,4},{12,20},{16,8},{20,24},{24,12},{28,28},{1,1},{5... | collective-permute-start | bytes 786440 | tf_op jit(solution)/shard_map/ppermute | solution.py:290
  12.9 18.3 %collective-permute-start.1 = (bf16[8,2,64,128]{3,2,1,0:T(8,128)(2,1)S(1)}, bf16[8,2,64,128]{3,2,1,0:T(8,128)(2,1)}, u32[]{:S(2)}, u32[]{:S(2)}) collective-permute-start(bf16[8,2,64,128]{3,2,1,0:T(8,128)(2,1)S(1)} %get-tuple-element.46), channel_id=1, source_target_pairs={{0,16},{4,0},{8,20},{12,4},{16,24},{20,8},{24,28},{28,12},{1,17},{... | collective-permute-start | bytes 786440 | tf_op jit(solution)/shard_map/ppermute | solution.py:290
  24.5 4.2 %copy-start.3 = (bf16[2,16,8,2048]{3,2,1,0:T(8,128)(2,1)S(1)}, bf16[2,16,8,2048]{3,2,1,0:T(8,128)(2,1)}, u32[]{:S(2)}) copy-start(bf16[2,16,8,2048]{3,2,1,0:T(8,128)(2,1)} %get-tuple-element.32) | copy-start | bytes 3145732
  24.5 4.2 %copy-start.4 = (bf16[2,16,8,2048]{3,2,1,0:T(8,128)(2,1)S(1)}, bf16[2,16,8,2048]{3,2,1,0:T(8,128)(2,1)}, u32[]{:S(2)}) copy-start(bf16[2,16,8,2048]{3,2,1,0:T(8,128)(2,1)} %get-tuple-element.33) | copy-start | bytes 3145732
  31.2 12.0 %copy-start.7 = (f32[2,512]{1,0:T(2,128)S(1)}, f32[2,512]{1,0:T(2,128)}, u32[]{:S(2)}) copy-start(f32[2,512]{1,0:T(2,128)} %param.15) | copy-start | bytes 12292
  33.1 10.3 %copy-start = (f32[2,2048]{1,0:T(2,128)S(1)}, f32[2,2048]{1,0:T(2,128)}, u32[]{:S(2)}) copy-start(f32[2,2048]{1,0:T(2,128)} %off_ref.1) | copy-start | bytes 49156
  33.1 10.4 %copy-start.1 = (s32[2048]{0:T(1024)S(1)}, s32[2048]{0:T(1024)}, u32[]{:S(2)}) copy-start(s32[2048]{0:T(1024)} %param.13) | copy-start | bytes 24580
  35.9 40.0 %collective-permute-start.10 = (bf16[8,2,16,2048]{3,2,1,0:T(8,128)(2,1)}, bf16[8,2,16,2048]{3,2,1,0:T(8,128)(2,1)}, u32[]{:S(2)}, u32[]{:S(2)}) collective-permute-start(bf16[8,2,16,2048]{3,2,1,0:T(8,128)(2,1)} %bitcast.32), channel_id=1, source_target_pairs={{0,8},{4,12},{8,0},{12,4},{16,24},{20,28},{24,16},{28,20},{1,9},{5... | collective-permute-start | bytes 3145736 | tf_op jit(solution)/shard_map/ppermute | solution.py:305
  40.0 45.4 %collective-permute-start.11 = (bf16[8,2,16,2048]{3,2,1,0:T(8,128)(2,1)}, bf16[8,2,16,2048]{3,2,1,0:T(8,128)(2,1)}, u32[]{:S(2)}, u32[]{:S(2)}) collective-permute-start(bf16[8,2,16,2048]{3,2,1,0:T(8,128)(2,1)} %bitcast.33), channel_id=1, source_target_pairs={{0,12},{4,8},{8,4},{12,0},{16,28},{20,24},{24,20},{28,16},{1,13},{... | collective-permute-start | bytes 3145736 | tf_op jit(solution)/shard_map/ppermute | solution.py:305
  40.6 48.7 %collective-permute-start.9 = (bf16[8,2,16,2048]{3,2,1,0:T(8,128)(2,1)S(1)}, bf16[8,2,16,2048]{3,2,1,0:T(8,128)(2,1)}, u32[]{:S(2)}, u32[]{:S(2)}) collective-permute-start(bf16[8,2,16,2048]{3,2,1,0:T(8,128)(2,1)S(1)} %bitcast.45), channel_id=1, source_target_pairs={{0,4},{4,0},{8,12},{12,8},{16,20},{20,16},{24,28},{28,24},{1,5},{5... | collective-permute-start | bytes 3145736 | tf_op jit(solution)/shard_map/ppermute | solution.py:305
  73.4 58.8 %collective-permute-start.2 = (bf16[8,2,16,2048]{3,2,1,0:T(8,128)(2,1)}, bf16[8,2,16,2048]{3,2,1,0:T(8,128)(2,1)S(1)}, u32[]{:S(2)}, u32[]{:S(2)}) collective-permute-start(bf16[8,2,16,2048]{3,2,1,0:T(8,128)(2,1)} %get-tuple-element.21), channel_id=1, source_target_pairs={{0,4},{4,0},{8,12},{12,8},{16,20},{20,16},{24,28},{28,24},{1,5},{5... | collective-permute-start | bytes 3145736 | tf_op jit(solution)/shard_map/ppermute | solution.py:305
  74.0 58.2 %collective-permute-start.3 = (bf16[8,2,16,2048]{3,2,1,0:T(8,128)(2,1)}, bf16[8,2,16,2048]{3,2,1,0:T(8,128)(2,1)}, u32[]{:S(2)}, u32[]{:S(2)}) collective-permute-start(bf16[8,2,16,2048]{3,2,1,0:T(8,128)(2,1)} %get-tuple-element.22), channel_id=1, source_target_pairs={{0,8},{4,12},{8,0},{12,4},{16,24},{20,28},{24,16},{28,20},{1,9},{5... | collective-permute-start | bytes 3145736 | tf_op jit(solution)/shard_map/ppermute | solution.py:305
  75.9 56.3 %collective-permute-start.4 = (bf16[8,2,16,2048]{3,2,1,0:T(8,128)(2,1)}, bf16[8,2,16,2048]{3,2,1,0:T(8,128)(2,1)}, u32[]{:S(2)}, u32[]{:S(2)}) collective-permute-start(bf16[8,2,16,2048]{3,2,1,0:T(8,128)(2,1)} %get-tuple-element.23), channel_id=1, source_target_pairs={{0,12},{4,8},{8,4},{12,0},{16,28},{20,24},{24,20},{28,16},{1,13},{... | collective-permute-start | bytes 3145736 | tf_op jit(solution)/shard_map/ppermute | solution.py:305
  122.6 46.2 %collective-permute-start.12 = (f32[8,128,128]{2,1,0:T(8,128)S(1)}, f32[8,128,128]{2,1,0:T(8,128)S(1)}, u32[]{:S(2)}, u32[]{:S(2)}) collective-permute-start(f32[8,128,128]{2,1,0:T(8,128)S(1)} %get-tuple-element.41), channel_id=1, source_target_pairs={{0,1},{1,0},{2,3},{3,2},{4,5},{5,4},{6,7},{7,6},{8,9},{9,8},{10,11... | collective-permute-start | bytes 1572872 | tf_op jit(solution)/shard_map/ppermute | solution.py:321
  122.6 46.6 %collective-permute-start.13 = (f32[8,128,128]{2,1,0:T(8,128)S(1)}, f32[8,128,128]{2,1,0:T(8,128)S(1)}, u32[]{:S(2)}, u32[]{:S(2)}) collective-permute-start(f32[8,128,128]{2,1,0:T(8,128)S(1)} %get-tuple-element.43), channel_id=1, source_target_pairs={{0,2},{1,3},{2,0},{3,1},{4,6},{5,7},{6,4},{7,5},{8,10},{9,11},{10,... | collective-permute-start | bytes 1572872 | tf_op jit(solution)/shard_map/ppermute | solution.py:321
  132.1 1.0 copy-start.8
  132.1 37.1 %collective-permute-start.14 = (f32[8,128,128]{2,1,0:T(8,128)S(1)}, f32[8,128,128]{2,1,0:T(8,128)}, u32[]{:S(2)}, u32[]{:S(2)}) collective-permute-start(f32[8,128,128]{2,1,0:T(8,128)S(1)} %get-tuple-element.42), channel_id=1, source_target_pairs={{0,3},{1,2},{2,1},{3,0},{4,7},{5,6},{6,5},{7,4},{8,11},{9,10},{10,... | collective-permute-start | bytes 1572872 | tf_op jit(solution)/shard_map/ppermute | solution.py:321
  167.2 35.0 %copy-start.2 = (f32[8,2,128,128]{3,2,1,0:T(8,128)S(1)}, f32[8,2,128,128]{3,2,1,0:T(8,128)}, u32[]{:S(2)}) copy-start(f32[8,2,128,128]{3,2,1,0:T(8,128)} %param.10) | copy-start | bytes 3145732
  167.2 4.9 %collective-permute-start.5 = (f32[8,128,128]{2,1,0:T(8,128)}, f32[8,128,128]{2,1,0:T(8,128)}, u32[]{:S(2)}, u32[]{:S(2)}) collective-permute-start(f32[8,128,128]{2,1,0:T(8,128)} %get-tuple-element.36), channel_id=1, source_target_pairs={{0,1},{1,0},{2,3},{3,2},{4,5},{5,4},{6,7},{7,6},{8,9},{9,8},{10,11... | collective-permute-start | bytes 1572872 | tf_op jit(solution)/shard_map/ppermute | solution.py:321
  167.9 15.1 %collective-permute-start.6 = (f32[8,128,128]{2,1,0:T(8,128)}, f32[8,128,128]{2,1,0:T(8,128)}, u32[]{:S(2)}, u32[]{:S(2)}) collective-permute-start(f32[8,128,128]{2,1,0:T(8,128)} %get-tuple-element.38), channel_id=1, source_target_pairs={{0,2},{1,3},{2,0},{3,1},{4,6},{5,7},{6,4},{7,5},{8,10},{9,11},{10,... | collective-permute-start | bytes 1572872 | tf_op jit(solution)/shard_map/ppermute | solution.py:321
  168.7 23.6 %collective-permute-start.7 = (f32[8,128,128]{2,1,0:T(8,128)}, f32[8,128,128]{2,1,0:T(8,128)}, u32[]{:S(2)}, u32[]{:S(2)}) collective-permute-start(f32[8,128,128]{2,1,0:T(8,128)} %get-tuple-element.37), channel_id=1, source_target_pairs={{0,3},{1,2},{2,1},{3,0},{4,7},{5,6},{6,5},{7,4},{8,11},{9,10},{10,... | collective-permute-start | bytes 1572872 | tf_op jit(solution)/shard_map/ppermute | solution.py:321
  170.6 54.4 %copy-start.9 = (f32[128]{0:T(128)S(1)}, f32[128]{0:T(128)}, u32[]{:S(2)}) copy-start(f32[128]{0:T(128)} %param.16) | copy-start | bytes 1540
  170.6 57.6 %copy-start.5 = (f32[8,2,128,128]{3,2,1,0:T(8,128)S(1)}, f32[8,2,128,128]{3,2,1,0:T(8,128)}, u32[]{:S(2)}) copy-start(f32[8,2,128,128]{3,2,1,0:T(8,128)} %param.11) | copy-start | bytes 3145732
  170.6 29.5 %collective-permute-start.15 = (f32[8,128,128]{2,1,0:T(8,128)S(1)}, f32[8,128,128]{2,1,0:T(8,128)S(1)}, u32[]{:S(2)}, u32[]{:S(2)}) collective-permute-start(f32[8,128,128]{2,1,0:T(8,128)S(1)} %add_multiply_fusion), channel_id=1, source_target_pairs={{16,0},{0,4},{20,8},{4,12},{24,16},{8,20},{28,24},{12,28},{17,1},{... | collective-permute-start | bytes 1572872 | tf_op jit(solution)/shard_map/ppermute | solution.py:322
  194.7 6.1 %collective-permute-start.8 = (f32[8,128,128]{2,1,0:T(8,128)}, f32[8,128,128]{2,1,0:T(8,128)}, u32[]{:S(2)}, u32[]{:S(2)}) collective-permute-start(f32[8,128,128]{2,1,0:T(8,128)} %add_multiply_fusion.1), channel_id=1, source_target_pairs={{0,0},{16,4},{4,8},{20,12},{8,16},{24,20},{12,24},{28,28},{1,1},{1... | collective-permute-start | bytes 1572872 | tf_op jit(solution)/shard_map/ppermute | solution.py:322
  200.1 0.8 copy-start.6
  202.4 16.2 %collective-permute-start.16 = (f32[128,128]{1,0:T(8,128)S(1)}, f32[128,128]{1,0:T(8,128)S(1)}, u32[]{:S(2)}, u32[]{:S(2)}) collective-permute-start(f32[128,128]{1,0:T(8,128)S(1)} %multiply_reduce_fusion), channel_id=1, source_target_pairs={{0,4},{4,0},{8,12},{12,8},{16,20},{20,16},{24,28},{28,24},{1,5},{5... | collective-permute-start | bytes 196616 | tf_op jit(solution)/shard_map/ppermute | solution.py:333
  218.6 4.3 %collective-permute-start.17 = (f32[128,128]{1,0:T(8,128)S(1)}, f32[128,128]{1,0:T(8,128)S(1)}, u32[]{:S(2)}, u32[]{:S(2)}) collective-permute-start(f32[128,128]{1,0:T(8,128)S(1)} %add.166), channel_id=1, source_target_pairs={{0,8},{4,12},{8,0},{12,4},{16,24},{20,28},{24,16},{28,20},{1,9},{5... | collective-permute-start | bytes 196616 | tf_op jit(solution)/shard_map/ppermute | solution.py:333
  222.9 5.2 %collective-permute-start.18 = (f32[128,128]{1,0:T(8,128)S(1)}, f32[128,128]{1,0:T(8,128)S(1)}, u32[]{:S(2)}, u32[]{:S(2)}) collective-permute-start(f32[128,128]{1,0:T(8,128)S(1)} %add.167), channel_id=1, source_target_pairs={{0,16},{4,20},{8,24},{12,28},{16,0},{20,4},{24,8},{28,12},{1,17},{... | collective-permute-start | bytes 196616 | tf_op jit(solution)/shard_map/ppermute | solution.py:333
Sparse Core Ops, SparseCore 0:
  33.2 23.2 all-gather.1

commit v4 on v3

--- a/solution.py
+++ b/solution.py
@@ -313,12 +313,12 @@
         partial = bins_gradient(
             place, trig[0:2], trig[2 * c + 2 : 2 * c + 4], iterate, observed[c], normalizer
         )
-        total = lax.dynamic_slice_in_dim(partial, mine * cell_share, cell_share, 2)
-        for d in range(1, sta_size):
-            sent = lax.dynamic_slice_in_dim(
-                partial, jnp.bitwise_xor(mine, d) * cell_share, cell_share, 2
-            )
-            total = total + lax.ppermute(sent, "sta", [(s, s ^ d) for s in range(sta_size)])
+        share = lambda d: lax.dynamic_slice_in_dim(
+            partial, jnp.bitwise_xor(mine, d) * cell_share, cell_share, 2
+        )
+        swap = lambda block, d: lax.ppermute(block, "sta", [(s, s ^ d) for s in range(sta_size)])
+        across = share(2) + swap(share(3), 1)
+        total = share(0) + swap(share(1), 1) + swap(across, 2)
         home = lax.ppermute(total * normalizer, "freq", gradient_back[c])
         halves.append(home.reshape(bins, 2, half_windows, cell_share))
     even = lax.rem(me, 2) == 0

time: 237 us -> 237 us (level)
  starting transfers between devices: 42 us -> 37.6 us
  other arithmetic: 10.1 us -> 12.6 us
    ppermute x2, starting transfers between devices: 6.85 us -> 2.9 us  [local_grouped(): home = lax.ppermute(total * normalizer, 'freq', gradient_back[c])]
    ppermute x6, waiting for transfers between devices: 20.2 us -> 17 us  [local_grouped(): lax.ppermute(block, 'sta', [(s, s ^ d) for s in range(sta_size)])]
    add x0 -> x2, other arithmetic: none -> 2.95 us  [local_grouped(): across = share(2) + swap(share(3), 1)]
    unnamed x26 -> x32, local copies, waits for them, and re-layouts: 9.37 us -> 8.51 us
  transfers between devices with their start and end apart: 20 -> 20, of which waited for: 8 -> 10; matrix products, arithmetic and copies ran while one was open for 14% -> 15% of each run, Pallas kernels for 39% -> 39%
where the time goes in v4:
time: 237 us
  Pallas kernels  91.5 us (39%)
  waiting for transfers between devices  48.9 us (21%)
  starting transfers between devices  37.6 us (16%)
  local copies, waits for them, and re-layouts  31.3 us (13%)
  between operations  14.9 us (6%)
  other arithmetic  12.6 us (5%)
    pallas_call x2, Pallas kernels, bins_gradient(): pl.pallas_call(functools.partial(bins_kernel, normalizer), grid=(stations...  63.2 us
    pallas_call x1, Pallas kernels, angles(): pl.pallas_call(functools.partial(angles_kernel, period), grid=(stations /...  28.4 us
    ppermute x6, waiting for transfers between devices, local_grouped(): lax.ppermute(parts[d], 'freq', [(f, f ^ d) for f in range(freq_size)])  20.5 us
    ppermute x3, starting transfers between devices, local_grouped(): lax.ppermute(squares, 'freq', [(f, f ^ d) for f in range(freq_size)])  17.1 us
    ppermute x6, waiting for transfers between devices, local_grouped(): lax.ppermute(block, 'sta', [(s, s ^ d) for s in range(sta_size)])  17 us
    ppermute x3, waiting for transfers between devices, local_grouped(): lax.ppermute(squares, 'freq', [(f, f ^ d) for f in range(freq_size)])  9.3 us
    dynamic_slice x1, local copies, waits for them, and re-layouts, local_grouped(): lax.dynamic_slice_in_dim(spectra, first, bins, 2).astype(jnp.bfloat16)  8.82 us
    unnamed x32, local copies, waits for them, and re-layouts  8.51 us
  transfers between devices with their start and end apart: 20, of which 10 were waited for; matrix products, arithmetic and copies ran while one was open for 15% of the time, Pallas kernels for 39%

profile of v4, /device:TPU:0, one launch (start us, length us, event | category | flops | bytes accessed | tf_op | source)
XLA Modules:
  0.0 236.8 jit_solution(2516016379379864089)
XLA Ops:
  7.2 1.3 convert_element_type.35
  8.6 0.7 constant_dynamic-slice_fusion.8
  9.3 3.6 %collective-permute-start = (bf16[8,2,64,128]{3,2,1,0:T(8,128)(2,1)}, bf16[8,2,64,128]{3,2,1,0:T(8,128)(2,1)}, u32[]{:S(2)}, u32[]{:S(2)}) collective-permute-start(bf16[8,2,64,128]{3,2,1,0:T(8,128)(2,1)} %get-tuple-element.45), channel_id=1, source_target_pairs={{0,0},{4,16},{8,4},{12,20},{16,8},{20,24},{24,12},{28,28},{1,1},{5... | collective-permute-start | bytes 786440 | tf_op jit(solution)/shard_map/ppermute | solution.py:290
  12.9 2.8 %collective-permute-start.1 = (bf16[8,2,64,128]{3,2,1,0:T(8,128)(2,1)S(1)}, bf16[8,2,64,128]{3,2,1,0:T(8,128)(2,1)}, u32[]{:S(2)}, u32[]{:S(2)}) collective-permute-start(bf16[8,2,64,128]{3,2,1,0:T(8,128)(2,1)S(1)} %get-tuple-element.44), channel_id=1, source_target_pairs={{0,16},{4,0},{8,20},{12,4},{16,24},{20,8},{24,28},{28,12},{1,17},{... | collective-permute-start | bytes 786440 | tf_op jit(solution)/shard_map/ppermute | solution.py:290
  15.7 8.8 %constant_dynamic-slice_fusion.2 = (bf16[2,16,8,2048]{3,2,1,0:T(8,128)(2,1)S(1)}, bf16[2,16,8,2048]{3,2,1,0:T(8,128)(2,1)}, bf16[2,16,8,2048]{3,2,1,0:T(8,128)(2...) fusion(f32[2,16,64,2048]{3,2,1,0:T(8,128)} %param.9, ...), kind=kLoop, calls=%fused_computation.33 | loop fusion | bytes 16777248 | tf_op jit(solution)/shard_map/dynamic_slice | solution.py:299
  24.6 4.2 %fusion = (bf16[8,2,16,2048]{3,2,1,0:T(8,128)(2,1)}, bf16[8,2,16,2048]{3,2,1,0:T(8,128)(2,1)}) fusion(bf16[2,16,8,2048]{3,2,1,0:T(8,128)(2,1)} %get-tuple-element.35, bf16[2,16,8,2048]{3,2,1,0:T(8,128)(2,1)} %get-tuple-element.34), kind=kLoop, calls=%fused_computation.8 | loop fusion | bytes 4194304 | tf_op jit(solution)/shard_map/transpose | solution.py:300
  28.8 2.5 %fusion.2 = (bf16[8,2,16,2048]{3,2,1,0:T(8,128)(2,1)}, bf16[8,2,16,2048]{3,2,1,0:T(8,128)(2,1)}) fusion(bf16[2,16,8,2048]{3,2,1,0:T(8,128)(2,1)S(1)} %copy-done.4, bf16[2,16,8,2048]{3,2,1,0:T(8,128)(2,1)S(1)} %copy-done.3), kind=kLoop, calls=%fused_computation.10 | loop fusion | bytes 4194304 | tf_op jit(solution)/shard_map/transpose | solution.py:300
  31.3 1.9 pad_maximum_fusion
  33.2 2.8 %copy.66 = bf16[2,16,8,2048]{3,1,0,2:T(8,128)(2,1)} copy(bf16[2,16,8,2048]{3,2,1,0:T(8,128)(2,1)} %get-tuple-element.29) | data formatting | bytes 2097152
  36.0 2.6 %collective-permute-start.10 = (bf16[8,2,16,2048]{3,2,1,0:T(8,128)(2,1)}, bf16[8,2,16,2048]{3,2,1,0:T(8,128)(2,1)}, u32[]{:S(2)}, u32[]{:S(2)}) collective-permute-start(bf16[8,2,16,2048]{3,2,1,0:T(8,128)(2,1)} %bitcast.32), channel_id=1, source_target_pairs={{0,8},{4,12},{8,0},{12,4},{16,24},{20,28},{24,16},{28,20},{1,9},{5... | collective-permute-start | bytes 3145736 | tf_op jit(solution)/shard_map/ppermute | solution.py:305
  38.6 1.5 copy.67
  40.1 0.6 copy.65
  40.7 1.5 collective-permute-start.9
  42.7 28.4 %shard_map.104 = (f32[512,2048]{1,0:T(8,128)}, f32[512,2048]{1,0:T(8,128)}, f32[512,2048]{1,0:T(8,128)}, f32[512,2048]{1,0:T(8,128)}, f32[512,2048]{1,0:T(8,128)}, /*index=5*/f32[512,2048]{1,0:T(8,128)}) custom-call(s32[2]{0:T(128)S(1)} %pad_add_fusion.numbers_ref, s32[1,2048]{1,0:T(1,128)S(1)} %bitcast.40, f32[2,2048]{1,0:T(2,128)S(1)} %copy-done, ...), custom_call_target="tpu_custom_call" | custom-call | flops 24999999488 | bytes 25165824 | tf_op jit(solution)/shard_map/pallas_call | solution.py:162
  71.0 1.5 copy.64
  72.6 0.6 collective-permute-start.2
  73.2 1.9 collective-permute-start.3
  75.1 1.1 collective-permute-start.4
  76.1 1.7 fusion.10
  77.9 7.6 %collective-permute-done.11.o3 = bf16[8,2,16,2048]{3,2,1,0:T(8,128)(2,1)} collective-permute-done((bf16[8,2,16,2048]{3,2,1,0:T(8,128)(2,1)}, bf16[8,2,16,2048]{3,2,1,0:T(8,128)(2,1)}, u32[]{:S(2)}, u32[]{:S(2)}) %collective-permute-start.11) | collective-permute-done | bytes 1048608 | tf_op jit(solution)/shard_map/ppermute | solution.py:305
  85.5 4.0 %collective-permute-done.9.o1 = bf16[8,2,16,2048]{3,2,1,0:T(8,128)(2,1)} collective-permute-done((bf16[8,2,16,2048]{3,2,1,0:T(8,128)(2,1)S(1)}, bf16[8,2,16,2048]{3,2,1,0:T(8,128)(2,1)}, u32[]{:S(2)}, u32[]{:S(2)}) %collective-permute-start.9) | collective-permute-done | bytes 1048608 | tf_op jit(solution)/shard_map/ppermute | solution.py:305
  89.5 31.6 %shard_map.106 = f32[8,128,512]{2,1,0:T(8,128)} custom-call(s32[1]{0:T(128)} %bitcast.place_ref, f32[512,2048]{1,0:T(8,128)} %get-tuple-element.14.uc_ref, f32[512,2048]{1,0:T(8,128)} %get-tuple-element.15.us_ref, f32[512,2048]{1,0:T(8,128)} %get-tuple-element.24.fc_ref, f32[512,2048]{1,0:T(8,128)} %get-tuple-element.25.fs_ref, ...), custom_call_target="tpu_custom_call" | custom-call | flops 8589934592 | bytes 16777216 | tf_op jit(solution)/shard_map/pallas_call | solution.py:244
  121.0 2.3 constant_dynamic-slice_fusion.1
  123.4 8.9 %collective-permute-done.2.o1 = bf16[8,2,16,2048]{3,2,1,0:T(8,128)(2,1)S(1)} collective-permute-done((bf16[8,2,16,2048]{3,2,1,0:T(8,128)(2,1)}, bf16[8,2,16,2048]{3,2,1,0:T(8,128)(2,1)S(1)}, u32[]{:S(2)}, u32[]{:S(2)}) %collective-permute-start.2) | collective-permute-done | bytes 1048608 | tf_op jit(solution)/shard_map/ppermute | solution.py:305
  132.3 1.0 copy-done.11
  133.2 31.6 %shard_map.105 = f32[8,128,512]{2,1,0:T(8,128)} custom-call(s32[1]{0:T(128)} %bitcast.place_ref, f32[512,2048]{1,0:T(8,128)} %get-tuple-element.14.uc_ref, f32[512,2048]{1,0:T(8,128)} %get-tuple-element.15.us_ref, f32[512,2048]{1,0:T(8,128)} %get-tuple-element.16.fc_ref, f32[512,2048]{1,0:T(8,128)} %get-tuple-element.17.fs_ref, ...), custom_call_target="tpu_custom_call" | custom-call | flops 8589934592 | bytes 16777216 | tf_op jit(solution)/shard_map/pallas_call | solution.py:244
  164.8 2.4 %constant_dynamic-slice_fusion.7 = (f32[8,128,128]{2,1,0:T(8,128)}, f32[8,128,128]{2,1,0:T(8,128)}) fusion(f32[8,128,512]{2,1,0:T(8,128)} %shard_map.105, s32[]{:T(128)S(6)} %select_n.85, s32[]{:T(128)S(6)} %select_n.87), kind=kLoop, calls=%fused_computation.38 | loop fusion | bytes 2097160 | tf_op jit(solution)/shard_map/dynamic_slice | solution.py:316
  167.2 0.5 collective-permute-start.12
  167.8 0.9 dynamic-slice_add_fusion
  168.7 1.5 collective-permute-start.14
  170.2 2.0 dynamic-slice_add_fusion.1
  172.3 1.5 collective-permute-start.7
  173.7 10.0 %collective-permute-done.14 = f32[8,128,128]{2,1,0:T(8,128)} collective-permute-done((f32[8,128,128]{2,1,0:T(8,128)}, f32[8,128,128]{2,1,0:T(8,128)}, u32[]{:S(2)}, u32[]{:S(2)}) %collective-permute-start.14) | collective-permute-done | bytes 524320 | tf_op jit(solution)/shard_map/ppermute | solution.py:319
  183.8 1.9 add_multiply_fusion
  185.7 1.5 collective-permute-start.15
  187.2 6.9 %collective-permute-done.7 = f32[8,128,128]{2,1,0:T(8,128)} collective-permute-done((f32[8,128,128]{2,1,0:T(8,128)}, f32[8,128,128]{2,1,0:T(8,128)}, u32[]{:S(2)}, u32[]{:S(2)}) %collective-permute-start.7) | collective-permute-done | bytes 524320 | tf_op jit(solution)/shard_map/ppermute | solution.py:319
  194.0 1.3 add_multiply_fusion.1
  195.3 1.4 collective-permute-start.8
  196.8 2.1 collective-permute-done.15
  198.9 0.8 copy-done.8
  199.7 1.3 broadcast_select_fusion.1
  201.1 14.0 %collective-permute-start.16 = (f32[128,128]{1,0:T(8,128)S(1)}, f32[128,128]{1,0:T(8,128)S(1)}, u32[]{:S(2)}, u32[]{:S(2)}) collective-permute-start(f32[128,128]{1,0:T(8,128)S(1)} %multiply_reduce_fusion), channel_id=1, source_target_pairs={{0,4},{4,0},{8,12},{12,8},{16,20},{20,16},{24,28},{28,24},{1,5},{5... | collective-permute-start | bytes 196616 | tf_op jit(solution)/shard_map/ppermute | solution.py:333
  215.1 2.2 collective-permute-done.16
  217.4 1.4 collective-permute-start.17
  218.7 3.6 %collective-permute-done.17 = f32[128,128]{1,0:T(8,128)S(1)} collective-permute-done((f32[128,128]{1,0:T(8,128)S(1)}, f32[128,128]{1,0:T(8,128)S(1)}, u32[]{:S(2)}, u32[]{:S(2)}) %collective-permute-start.17) | collective-permute-done | bytes 65568 | tf_op jit(solution)/shard_map/ppermute | solution.py:333
  222.3 1.7 collective-permute-start.18
  224.8 3.5 %collective-permute-done.18 = f32[128,128]{1,0:T(8,128)S(1)} collective-permute-done((f32[128,128]{1,0:T(8,128)S(1)}, f32[128,128]{1,0:T(8,128)S(1)}, u32[]{:S(2)}, u32[]{:S(2)}) %collective-permute-start.18) | collective-permute-done | bytes 65568 | tf_op jit(solution)/shard_map/ppermute | solution.py:333
  228.3 1.6 multiply_add_fusion
  (50 shorter events, 0.8 us)
Async XLA Ops:
  7.2 69.0 %all-gather.2.cloned.1.call-start = ((), (), s32[]{:S(2)}) async-start(), calls=%async_computation | async-start | bytes 2621440 | tf_op jit(solution)/shard_map/all_gather | solution.py:303
  9.3 22.0 %collective-permute-start = (bf16[8,2,64,128]{3,2,1,0:T(8,128)(2,1)}, bf16[8,2,64,128]{3,2,1,0:T(8,128)(2,1)}, u32[]{:S(2)}, u32[]{:S(2)}) collective-permute-start(bf16[8,2,64,128]{3,2,1,0:T(8,128)(2,1)} %get-tuple-element.45), channel_id=1, source_target_pairs={{0,0},{4,16},{8,4},{12,20},{16,8},{20,24},{24,12},{28,28},{1,1},{5... | collective-permute-start | bytes 786440 | tf_op jit(solution)/shard_map/ppermute | solution.py:290
  12.9 18.4 %collective-permute-start.1 = (bf16[8,2,64,128]{3,2,1,0:T(8,128)(2,1)S(1)}, bf16[8,2,64,128]{3,2,1,0:T(8,128)(2,1)}, u32[]{:S(2)}, u32[]{:S(2)}) collective-permute-start(bf16[8,2,64,128]{3,2,1,0:T(8,128)(2,1)S(1)} %get-tuple-element.44), channel_id=1, source_target_pairs={{0,16},{4,0},{8,20},{12,4},{16,24},{20,8},{24,28},{28,12},{1,17},{... | collective-permute-start | bytes 786440 | tf_op jit(solution)/shard_map/ppermute | solution.py:290
  24.6 4.2 %copy-start.3 = (bf16[2,16,8,2048]{3,2,1,0:T(8,128)(2,1)S(1)}, bf16[2,16,8,2048]{3,2,1,0:T(8,128)(2,1)}, u32[]{:S(2)}) copy-start(bf16[2,16,8,2048]{3,2,1,0:T(8,128)(2,1)} %get-tuple-element.32) | copy-start | bytes 3145732
  24.6 4.2 %copy-start.4 = (bf16[2,16,8,2048]{3,2,1,0:T(8,128)(2,1)S(1)}, bf16[2,16,8,2048]{3,2,1,0:T(8,128)(2,1)}, u32[]{:S(2)}) copy-start(bf16[2,16,8,2048]{3,2,1,0:T(8,128)(2,1)} %get-tuple-element.33) | copy-start | bytes 3145732
  36.0 39.1 %collective-permute-start.10 = (bf16[8,2,16,2048]{3,2,1,0:T(8,128)(2,1)}, bf16[8,2,16,2048]{3,2,1,0:T(8,128)(2,1)}, u32[]{:S(2)}, u32[]{:S(2)}) collective-permute-start(bf16[8,2,16,2048]{3,2,1,0:T(8,128)(2,1)} %bitcast.32), channel_id=1, source_target_pairs={{0,8},{4,12},{8,0},{12,4},{16,24},{20,28},{24,16},{28,20},{1,9},{5... | collective-permute-start | bytes 3145736 | tf_op jit(solution)/shard_map/ppermute | solution.py:305
  38.6 3.7 %copy-start.9 = (s32[64,512]{1,0:T(8,128)S(1)}, s32[64,512]{1,0:T(8,128)}, u32[]{:S(2)}) copy-start(s32[64,512]{1,0:T(8,128)} %param.12) | copy-start | bytes 393220
  38.6 3.8 %copy-start.10 = (f32[2,512]{1,0:T(2,128)S(1)}, f32[2,512]{1,0:T(2,128)}, u32[]{:S(2)}) copy-start(f32[2,512]{1,0:T(2,128)} %param.15) | copy-start | bytes 12292
  40.1 2.5 %copy-start = (f32[2,2048]{1,0:T(2,128)S(1)}, f32[2,2048]{1,0:T(2,128)}, u32[]{:S(2)}) copy-start(f32[2,2048]{1,0:T(2,128)} %off_ref.1) | copy-start | bytes 49156
  40.1 2.5 %copy-start.1 = (s32[2048]{0:T(1024)S(1)}, s32[2048]{0:T(1024)}, u32[]{:S(2)}) copy-start(s32[2048]{0:T(1024)} %param.13) | copy-start | bytes 24580
  40.1 45.3 %collective-permute-start.11 = (bf16[8,2,16,2048]{3,2,1,0:T(8,128)(2,1)}, bf16[8,2,16,2048]{3,2,1,0:T(8,128)(2,1)}, u32[]{:S(2)}, u32[]{:S(2)}) collective-permute-start(bf16[8,2,16,2048]{3,2,1,0:T(8,128)(2,1)} %bitcast.33), channel_id=1, source_target_pairs={{0,12},{4,8},{8,4},{12,0},{16,28},{20,24},{24,20},{28,16},{1,13},{... | collective-permute-start | bytes 3145736 | tf_op jit(solution)/shard_map/ppermute | solution.py:305
  40.7 48.7 %collective-permute-start.9 = (bf16[8,2,16,2048]{3,2,1,0:T(8,128)(2,1)S(1)}, bf16[8,2,16,2048]{3,2,1,0:T(8,128)(2,1)}, u32[]{:S(2)}, u32[]{:S(2)}) collective-permute-start(bf16[8,2,16,2048]{3,2,1,0:T(8,128)(2,1)S(1)} %bitcast.45), channel_id=1, source_target_pairs={{0,4},{4,0},{8,12},{12,8},{16,20},{20,16},{24,28},{28,24},{1,5},{5... | collective-permute-start | bytes 3145736 | tf_op jit(solution)/shard_map/ppermute | solution.py:305
  71.0 4.0 %copy-start.7 = (bf16[8,2,16,2048]{3,2,1,0:T(8,128)(2,1)S(1)}, bf16[8,2,16,2048]{3,2,1,0:T(8,128)(2,1)}, u32[]{:S(2)}) copy-start(bf16[8,2,16,2048]{3,2,1,0:T(8,128)(2,1)} %get-tuple-element.23) | copy-start | bytes 3145732
  72.6 59.7 %collective-permute-start.2 = (bf16[8,2,16,2048]{3,2,1,0:T(8,128)(2,1)}, bf16[8,2,16,2048]{3,2,1,0:T(8,128)(2,1)S(1)}, u32[]{:S(2)}, u32[]{:S(2)}) collective-permute-start(bf16[8,2,16,2048]{3,2,1,0:T(8,128)(2,1)} %get-tuple-element.21), channel_id=1, source_target_pairs={{0,4},{4,0},{8,12},{12,8},{16,20},{20,16},{24,28},{28,24},{1,5},{5... | collective-permute-start | bytes 3145736 | tf_op jit(solution)/shard_map/ppermute | solution.py:305
  73.2 59.1 %collective-permute-start.3 = (bf16[8,2,16,2048]{3,2,1,0:T(8,128)(2,1)}, bf16[8,2,16,2048]{3,2,1,0:T(8,128)(2,1)}, u32[]{:S(2)}, u32[]{:S(2)}) collective-permute-start(bf16[8,2,16,2048]{3,2,1,0:T(8,128)(2,1)} %get-tuple-element.22), channel_id=1, source_target_pairs={{0,8},{4,12},{8,0},{12,4},{16,24},{20,28},{24,16},{28,20},{1,9},{5... | collective-permute-start | bytes 3145736 | tf_op jit(solution)/shard_map/ppermute | solution.py:305
  75.1 57.2 %collective-permute-start.4 = (bf16[8,2,16,2048]{3,2,1,0:T(8,128)(2,1)S(1)}, bf16[8,2,16,2048]{3,2,1,0:T(8,128)(2,1)}, u32[]{:S(2)}, u32[]{:S(2)}) collective-permute-start(bf16[8,2,16,2048]{3,2,1,0:T(8,128)(2,1)S(1)} %copy-done.7), channel_id=1, source_target_pairs={{0,12},{4,8},{8,4},{12,0},{16,28},{20,24},{24,20},{28,16},{1,13},{... | collective-permute-start | bytes 3145736 | tf_op jit(solution)/shard_map/ppermute | solution.py:305
  123.3 44.4 %collective-permute-start.13 = (f32[8,128,128]{2,1,0:T(8,128)}, f32[8,128,128]{2,1,0:T(8,128)S(1)}, u32[]{:S(2)}, u32[]{:S(2)}) collective-permute-start(f32[8,128,128]{2,1,0:T(8,128)} %get-tuple-element.41), channel_id=1, source_target_pairs={{0,1},{1,0},{2,3},{3,2},{4,5},{5,4},{6,7},{7,6},{8,9},{9,8},{10,11... | collective-permute-start | bytes 1572872 | tf_op jit(solution)/shard_map/ppermute | solution.py:319
  132.3 1.0 copy-start.11
  164.8 2.9 %copy-start.5 = (f32[8,128,512]{2,1,0:T(8,128)S(1)}, f32[8,128,512]{2,1,0:T(8,128)}, u32[]{:S(2)}) copy-start(f32[8,128,512]{2,1,0:T(8,128)} %shard_map.106) | copy-start | bytes 6291460
  167.2 3.0 %collective-permute-start.6 = (f32[8,128,128]{2,1,0:T(8,128)}, f32[8,128,128]{2,1,0:T(8,128)}, u32[]{:S(2)}, u32[]{:S(2)}) collective-permute-start(f32[8,128,128]{2,1,0:T(8,128)} %get-tuple-element.37), channel_id=1, source_target_pairs={{0,1},{1,0},{2,3},{3,2},{4,5},{5,4},{6,7},{7,6},{8,9},{9,8},{10,11... | collective-permute-start | bytes 1572872 | tf_op jit(solution)/shard_map/ppermute | solution.py:319
  167.2 6.5 %collective-permute-start.12 = (f32[8,128,128]{2,1,0:T(8,128)}, f32[8,128,128]{2,1,0:T(8,128)S(1)}, u32[]{:S(2)}, u32[]{:S(2)}) collective-permute-start(f32[8,128,128]{2,1,0:T(8,128)} %get-tuple-element.40), channel_id=1, source_target_pairs={{0,1},{1,0},{2,3},{3,2},{4,5},{5,4},{6,7},{7,6},{8,9},{9,8},{10,11... | collective-permute-start | bytes 1572872 | tf_op jit(solution)/shard_map/ppermute | solution.py:319
  168.7 15.1 %collective-permute-start.14 = (f32[8,128,128]{2,1,0:T(8,128)}, f32[8,128,128]{2,1,0:T(8,128)}, u32[]{:S(2)}, u32[]{:S(2)}) collective-permute-start(f32[8,128,128]{2,1,0:T(8,128)} %dynamic-slice_add_fusion), channel_id=1, source_target_pairs={{0,2},{1,3},{2,0},{3,1},{4,6},{5,7},{6,4},{7,5},{8,10},{9,11},{10,... | collective-permute-start | bytes 1572872 | tf_op jit(solution)/shard_map/ppermute | solution.py:319
  170.1 17.0 %collective-permute-start.5 = (f32[8,128,128]{2,1,0:T(8,128)}, f32[8,128,128]{2,1,0:T(8,128)S(1)}, u32[]{:S(2)}, u32[]{:S(2)}) collective-permute-start(f32[8,128,128]{2,1,0:T(8,128)} %get-tuple-element.36), channel_id=1, source_target_pairs={{0,1},{1,0},{2,3},{3,2},{4,5},{5,4},{6,7},{7,6},{8,9},{9,8},{10,11... | collective-permute-start | bytes 1572872 | tf_op jit(solution)/shard_map/ppermute | solution.py:319
  172.3 21.8 %collective-permute-start.7 = (f32[8,128,128]{2,1,0:T(8,128)}, f32[8,128,128]{2,1,0:T(8,128)}, u32[]{:S(2)}, u32[]{:S(2)}) collective-permute-start(f32[8,128,128]{2,1,0:T(8,128)} %dynamic-slice_add_fusion.1), channel_id=1, source_target_pairs={{0,2},{1,3},{2,0},{3,1},{4,6},{5,7},{6,4},{7,5},{8,10},{9,11},{10,... | collective-permute-start | bytes 1572872 | tf_op jit(solution)/shard_map/ppermute | solution.py:319
  185.7 15.3 %copy-start.2 = (f32[8,2,128,128]{3,2,1,0:T(8,128)S(1)}, f32[8,2,128,128]{3,2,1,0:T(8,128)}, u32[]{:S(2)}) copy-start(f32[8,2,128,128]{3,2,1,0:T(8,128)} %param.10) | copy-start | bytes 3145732
  185.7 13.2 %collective-permute-start.15 = (f32[8,128,128]{2,1,0:T(8,128)}, f32[8,128,128]{2,1,0:T(8,128)S(1)}, u32[]{:S(2)}, u32[]{:S(2)}) collective-permute-start(f32[8,128,128]{2,1,0:T(8,128)} %add_multiply_fusion), channel_id=1, source_target_pairs={{16,0},{0,4},{20,8},{4,12},{24,16},{8,20},{28,24},{12,28},{17,1},{... | collective-permute-start | bytes 1572872 | tf_op jit(solution)/shard_map/ppermute | solution.py:322
  195.3 4.3 %collective-permute-start.8 = (f32[8,128,128]{2,1,0:T(8,128)S(1)}, f32[8,128,128]{2,1,0:T(8,128)}, u32[]{:S(2)}, u32[]{:S(2)}) collective-permute-start(f32[8,128,128]{2,1,0:T(8,128)S(1)} %add_multiply_fusion.1), channel_id=1, source_target_pairs={{0,0},{16,4},{4,8},{20,12},{8,16},{24,20},{12,24},{28,28},{1,1},{1... | collective-permute-start | bytes 1572872 | tf_op jit(solution)/shard_map/ppermute | solution.py:322
  196.8 27.3 %copy-start.12 = (f32[128]{0:T(128)S(1)}, f32[128]{0:T(128)}, u32[]{:S(2)}) copy-start(f32[128]{0:T(128)} %param.16) | copy-start | bytes 1540
  196.8 31.5 %copy-start.6 = (f32[8,2,128,128]{3,2,1,0:T(8,128)S(1)}, f32[8,2,128,128]{3,2,1,0:T(8,128)}, u32[]{:S(2)}) copy-start(f32[8,2,128,128]{3,2,1,0:T(8,128)} %param.11) | copy-start | bytes 3145732
  198.9 0.8 copy-start.8
  201.1 16.2 %collective-permute-start.16 = (f32[128,128]{1,0:T(8,128)S(1)}, f32[128,128]{1,0:T(8,128)S(1)}, u32[]{:S(2)}, u32[]{:S(2)}) collective-permute-start(f32[128,128]{1,0:T(8,128)S(1)} %multiply_reduce_fusion), channel_id=1, source_target_pairs={{0,4},{4,0},{8,12},{12,8},{16,20},{20,16},{24,28},{28,24},{1,5},{5... | collective-permute-start | bytes 196616 | tf_op jit(solution)/shard_map/ppermute | solution.py:333
  217.4 5.0 %collective-permute-start.17 = (f32[128,128]{1,0:T(8,128)S(1)}, f32[128,128]{1,0:T(8,128)S(1)}, u32[]{:S(2)}, u32[]{:S(2)}) collective-permute-start(f32[128,128]{1,0:T(8,128)S(1)} %add.166), channel_id=1, source_target_pairs={{0,8},{4,12},{8,0},{12,4},{16,24},{20,28},{24,16},{28,20},{1,9},{5... | collective-permute-start | bytes 196616 | tf_op jit(solution)/shard_map/ppermute | solution.py:333
  222.3 5.9 %collective-permute-start.18 = (f32[128,128]{1,0:T(8,128)S(1)}, f32[128,128]{1,0:T(8,128)S(1)}, u32[]{:S(2)}, u32[]{:S(2)}) collective-permute-start(f32[128,128]{1,0:T(8,128)S(1)} %add.167), channel_id=1, source_target_pairs={{0,16},{4,20},{8,24},{12,28},{16,0},{20,4},{24,8},{28,12},{1,17},{... | collective-permute-start | bytes 196616 | tf_op jit(solution)/shard_map/ppermute | solution.py:333
Sparse Core Ops, SparseCore 0:
  33.3 23.2 all-gather.1
